TPU v7x, 32 devices: a whole 2x2x4 slice. The times are simulated.
32 devices in a mesh: gx: 4 (over x, core), gy: 8 (over z, y).
Axes of the slice: x: 2, y: 2, z: 4, core: 2. Of those that a mesh axis runs over, the one named last changes fastest.
Arguments:
- fields_old: float32 [4096, 5, 512], P(('gx', 'gy')), may hold values from -6 to 6
- new_place: int32 [4096], P(('gx', 'gy')), may hold values from 0 to 4095, as said below
- box_slot: int32 [32, 128], P(('gx', 'gy')), may hold values from 0 to 127, each once within a row
- coarse_fields: float32 [1024, 5, 512], P(('gx', 'gy')), may hold values from -6 to 6
- coarse_source: int32 [32, 32], P(('gx', 'gy')), may hold values from 0 to 1023, as said below
- diffusivity: float32 [5], replicated, may hold values from 0.02 to 0.08
- velocity: float32 [3], replicated, may hold values from -0.15 to 0.15
Outputs:
- fields_new: float32 [4096, 5, 512], P(('gx', 'gy'))
Inputs may be any that keep to these rules, and one draw needn't show every extreme that they name: `new_place`: A permutation of the patch numbers. One device sends at most 8 patches to any one device, and exactly 8 to some. `box_slot`: each row is a permutation. `coarse_source`: coarse patch c is held by device c // 32; the patches that a device names are held by the devices with its gy index; every coarse patch is named once over all devices; exactly 8 entries of a device name patches of each such owner.
All inputs are finite; a program needn't handle non-finite values.
Results may differ from a plain program's by a relative error of at most 0.00002.
Values sent between devices are 32-bit elements; how exact they have to be, the bound alone decides.
A program may use at most 128 MiB of HBM per device.

v0:
```python
import jax
import jax.numpy as jnp
from jax import lax
from jax.sharding import PartitionSpec as P

S = 8
BX = 4
BY = 16
BZ = 2
SECTIONS = 4


def padded_2(value, sides, width):
    for axis, dim in sides:
        count, length = (lax.axis_size(axis), value.shape[dim])
        up = [(i, (i + 1) % count) for i in range(count)]
        down = [(j, i) for i, j in up]
        last = lax.slice_in_dim(value, length - width, length, axis=dim)
        initial = lax.slice_in_dim(value, 0, width, axis=dim)
        before = lax.ppermute(last, axis, up)
        after = lax.ppermute(initial, axis, down)
        value = jnp.concatenate([before, value, after], axis=dim)
    return value


def before_count(groups):
    length = groups.shape[0]
    indices = jnp.arange(length, dtype=jnp.int32)
    matched = (groups[:, None] == groups[None, :]) & (indices[:, None] < indices[None, :])
    return jnp.sum(matched.astype(jnp.int32), axis=0)


def to_grid(patch_rows, extent):
    field_count = patch_rows.shape[1]
    blocks = patch_rows.reshape(BZ, BX, BY, field_count, extent, extent, extent)
    return blocks.transpose(3, 0, 4, 1, 5, 2, 6).reshape(
        field_count, BZ * extent, BX * extent, BY * extent
    )


def from_grid(fine_grid, extent):
    field_count = fine_grid.shape[0]
    blocks = fine_grid.reshape(field_count, BZ, extent, BX, extent, BY, extent)
    return blocks.transpose(1, 3, 5, 0, 2, 4, 6).reshape(
        BZ * BX * BY, field_count, extent * extent * extent
    )


def refine(values, extent):
    values = values.reshape(values.shape[0], values.shape[1], extent, extent)
    return jnp.repeat(jnp.repeat(values, 2, axis=2), 2, axis=3)


def shifted(values, direction, offset):
    window = [slice(1, -1), slice(1, -1), slice(1, -1)]
    window[direction] = slice(offset, offset + values.shape[direction] - 2)
    return values[tuple(window)]


def update_field(padded, thermal, diffusivity, velocity):
    coefficient = diffusivity * thermal
    middle = shifted(padded, 0, 1)
    coef_mid = shifted(coefficient, 0, 1)
    updated = middle
    for direction in range(3):
        forward = shifted(padded, direction, 2)
        behind = shifted(padded, direction, 0)
        coef_up = shifted(coefficient, direction, 2)
        coef_down = shifted(coefficient, direction, 0)
        drift_speed = velocity[direction]
        updated = (
            updated
            + 0.5 * (coef_mid + coef_up) * (forward - middle)
            - 0.5 * (coef_mid + coef_down) * (middle - behind)
        )
        updated = updated - (
            jnp.maximum(drift_speed, 0.0) * (middle - behind)
            + jnp.minimum(drift_speed, 0.0) * (forward - middle)
        )
    return updated


def advance(lateral, planes, diffusivity, velocity):
    cap_planes = jnp.pad(planes, ((0, 0), (0, 0), (1, 1), (1, 1)))
    padded = jnp.concatenate([cap_planes[0][:, None], lateral, cap_planes[1][:, None]], axis=1)
    thermal = 1.0 + 0.5 * jnp.tanh(padded[0])
    return jax.vmap(update_field, in_axes=(0, None, 0, None))(
        padded, thermal, diffusivity, velocity
    )


def per_device(
    fields_old, new_place, box_slot, coarse_fields, coarse_source, diffusivity, velocity
):
    devices = lax.axis_size(("gx", "gy"))
    mesh_x = lax.axis_size("gx")
    mesh_y = lax.axis_size("gy")
    patches = fields_old.shape[0]
    extent = S
    cell_shape = fields_old.shape[1:]
    capacity = 2 * patches // devices
    destination = new_place // patches
    new_slot = new_place % patches
    position = destination * capacity + before_count(destination)
    outgoing = (
        jnp.zeros((devices * capacity,) + cell_shape, jnp.float32).at[position].set(fields_old)
    )
    slot_tags = jnp.full((devices * capacity,), -1, jnp.int32).at[position].set(new_slot)
    arrived, labels = (
        lax.all_to_all(outgoing, ("gx", "gy"), split_axis=0, concat_axis=0, tiled=True),
        lax.all_to_all(slot_tags, ("gx", "gy"), split_axis=0, concat_axis=0, tiled=True),
    )
    block_pos = box_slot[0]
    target = jnp.where(labels >= 0, block_pos[jnp.maximum(labels, 0)], patches)
    placed = jnp.zeros(fields_old.shape, jnp.float32).at[target].set(arrived, mode="drop")
    fine_grid = to_grid(placed, extent)
    source = coarse_source[0]
    need_count = source.shape[0]
    per_owner = need_count // mesh_x
    owners = source // need_count
    owner_column = owners // mesh_y
    coarse_slot = source % need_count
    upper_half = (jnp.arange(need_count, dtype=jnp.int32) >= need_count // 2).astype(jnp.int32)
    reply_row = owner_column * per_owner + before_count(owner_column)
    requests = (
        jnp.full((mesh_x * per_owner,), -1, jnp.int32)
        .at[reply_row]
        .set(coarse_slot * 2 + upper_half)
    )
    incoming = lax.all_to_all(requests, "gx", split_axis=0, concat_axis=0, tiled=True)
    field_count = coarse_fields.shape[1]
    coarse_layered = coarse_fields.reshape(
        coarse_fields.shape[0], field_count, extent, extent * extent
    )
    is_valid = (incoming >= 0)[:, None, None]
    wanted = jnp.maximum(incoming, 0)
    chosen = wanted // 2
    is_upper = wanted % 2
    top_layer = extent - 1
    near_layer = jnp.where(is_upper == 1, 0, top_layer)
    far_layer = jnp.where(is_upper == 1, 1, top_layer - 1)
    nearest = jnp.where(is_valid, coarse_layered[chosen, :, near_layer, :], 0.0)
    farther = jnp.where(is_valid, coarse_layered[chosen, :, far_layer, :], 0.0)
    values = 1.25 * nearest - 0.25 * farther
    returned = lax.all_to_all(values, "gx", split_axis=0, concat_axis=0, tiled=True)
    own_ghosts = refine(returned[reply_row], extent)
    own_ghosts = own_ghosts.reshape(2, BX // 2, BY // 2, field_count, 2 * extent, 2 * extent)
    planes = own_ghosts.transpose(0, 3, 1, 4, 2, 5).reshape(
        2, field_count, BX * extent, BY * extent
    )
    for section_no in range(SECTIONS):
        lateral = padded_2(fine_grid, (("gx", 2), ("gy", 3)), 1)
        fine_grid = advance(lateral, planes, diffusivity, velocity)
    patch_rows = from_grid(fine_grid, extent)
    return patch_rows[block_pos]


def solution(mesh):
    in_specs = (
        P(("gx", "gy"), None, None),
        P(("gx", "gy")),
        P(("gx", "gy"), None),
        P(("gx", "gy"), None, None),
        P(("gx", "gy"), None),
        P(),
        P(),
    )
    out_specs = P(("gx", "gy"), None, None)
    return jax.shard_map(
        per_device, mesh=mesh, in_specs=in_specs, out_specs=out_specs, check_vma=False
    )
```

profile of v0, /device:TPU:0, one launch (start us, length us, event | category | flops | bytes accessed | tf_op | source)
XLA Modules:
  0.0 376.5 jit_solution(573722860733252761)
XLA Ops:
  3.5 4.2 %all-to-all-start.2 = ((s32[4,8,1]{1,2,0:T(1,128)}), s32[4,8,1]{1,2,0:T(1,128)S(1)}, u32[]{:S(2)}, u32[]{:S(2)}) async-start(s32[4,8,1]{1,2,0:T(1,128)} %bitcast.10), calls=%async_computation.2 | async-start | bytes 4096 | tf_op jit(solution)/shard_map/all_to_all | solution.py:130
  11.4 5.5 %all-to-all-start = ((s32[32,8,1]{1,2,0:T(1,128)}), s32[32,8,1]{1,2,0:T(1,128)S(1)}, u32[]{:S(2)}, u32[]{:S(2)}) async-start(s32[32,8,1]{1,2,0:T(1,128)} %bitcast), calls=%async_computation | async-start | bytes 32768 | tf_op jit(solution)/shard_map/all_to_all | solution.py:111
  19.0 2.5 broadcast_in_dim.43
  21.6 15.7 %scatter_fusion = f32[256,5,512]{2,1,0:T(8,128)} fusion(f32[256,5,512]{2,1,0:T(8,128)} %broadcast_in_dim.43, s32[128]{0:T(128)S(1)} %compare_select_fusion.4, f32[128,5,512]{2,1,0:T(8,128)S(1)} %copy.143), kind=kCustom, calls=%fused_computation.6 | custom fusion | bytes 3932672 | tf_op jit(solution)/shard_map/scatter | solution.py:106
  37.3 6.0 %all-to-all-start.1 = ((f32[256,5,512]{2,1,0:T(8,128)}), f32[256,5,512]{2,1,0:T(8,128)}, u32[]{:S(2)}, u32[]{:S(2)}) async-start(f32[256,5,512]{2,1,0:T(8,128)} %scatter_fusion), calls=%async_computation.1 | async-start | bytes 8388608 | tf_op jit(solution)/shard_map/all_to_all | solution.py:110
  49.4 89.8 %all-to-all-done.1 = f32[256,5,512]{2,1,0:T(8,128)} async-done(((f32[256,5,512]{2,1,0:T(8,128)}), f32[256,5,512]{2,1,0:T(8,128)}, u32[]{:S(2)}, u32[]{:S(2)}) %all-to-all-start.1) | async-done | bytes 2621472 | tf_op jit(solution)/shard_map/all_to_all | solution.py:110
  139.3 3.3 all-to-all-start.3
  142.8 22.3 %scatter_fusion.1 = f32[128,5,512]{2,1,0:T(8,128)S(1)} fusion(f32[128,5,512]{2,1,0:T(8,128)S(1)} %broadcast_in_dim.40, s32[256]{0:T(256)S(1)} %bitcast.93, f32[256,5,512]{2,1,0:T(8,128)} %all-to-all-done.1), kind=kCustom, calls=%fused_computation.7 | custom fusion | bytes 7865344 | tf_op jit(solution)/shard_map/scatter | solution.py:115
  165.8 8.5 %reshape.344 = f32[2,4,16,5,8,8,8]{2,1,0,6,5,4,3:T(4,128)} reshape(f32[128,5,512]{0,2,1:T(8,128)S(1)} %copy.144) | data formatting | bytes 2621440 | tf_op jit(solution)/shard_map/reshape | solution.py:35
  174.3 17.3 %copy.145 = f32[5,2,8,4,8,16,8]{6,5,4,3,2,1,0:T(8,128)} copy(f32[5,2,8,4,8,16,8]{5,3,1,6,4,2,0:T(4,128)} %bitcast.89) | data formatting | bytes 2621440 | tf_op jit(solution)/shard_map/transpose | solution.py:36
  191.6 14.4 %reshape.345 = f32[5,16,32,128]{3,2,1,0:T(8,128)S(1)} reshape(f32[5,2,8,4,8,16,8]{6,5,4,3,2,1,0:T(8,128)} %copy.145) | data formatting | bytes 2621440 | tf_op jit(solution)/shard_map/reshape | solution.py:36
  218.5 2.2 fusion.151
  225.0 4.7 %collective-permute-start.3 = (f32[5,16,34,1]{2,1,3,0:T(8,128)S(1)}, f32[5,16,34,1]{2,1,3,0:T(8,128)S(1)}, u32[]{:S(2)}, u32[]{:S(2)}) collective-permute-start(f32[5,16,34,1]{2,1,3,0:T(8,128)S(1)} %copy.153), channel_id=1, source_target_pairs={{1,0},{2,1},{3,2},{4,3},{5,4},{6,5},{7,6},{0,7},{9,8},{10,9},{11,1... | collective-permute-start | bytes 32648 | tf_op jit(solution)/shard_map/ppermute | solution.py:21
  237.1 6.3 %fusion.87 = f32[5,16,32,128]{3,2,1,0:T(8,128)S(1)} fusion(f32[5,18,34,130]{3,2,1,0:T(8,128)S(1)} %broadcast_multiply_fusion.3, f32[5,16,32,128]{3,2,1,0:T(8,128)S(1)} %reshape.345, f32[5,16,34,1]{3,2,1,0:T(8,128)S(1)} %copy-done.6, f32[5,16,1,128]{3,2,1,0:T(1,128)S(1)} %collective-permute-done.1, f32[5,16,1,128]{3,2,1,0:T(1,128)S(1)} %collective-permute-done, ...), kind=kLoop, calls=%fused_computation.190 | loop fusion | flops 19660800 | bytes 12076984 | tf_op jit(solution)/shard_map/vmap()/sub | solution.py:76
  253.7 4.7 %collective-permute-start.7 = (f32[5,16,34,1]{2,1,3,0:T(8,128)S(1)}, f32[5,16,34,1]{2,1,3,0:T(8,128)S(1)}, u32[]{:S(2)}, u32[]{:S(2)}) collective-permute-start(f32[5,16,34,1]{2,1,3,0:T(8,128)S(1)} %copy.161), channel_id=1, source_target_pairs={{1,0},{2,1},{3,2},{4,3},{5,4},{6,5},{7,6},{0,7},{9,8},{10,9},{11,1... | collective-permute-start | bytes 32648 | tf_op jit(solution)/shard_map/ppermute | solution.py:21
  265.6 6.3 %fusion.62 = f32[5,16,32,128]{3,2,1,0:T(8,128)S(1)} fusion(f32[5,18,34,130]{3,2,1,0:T(8,128)S(1)} %broadcast_multiply_fusion.2, f32[5,16,32,128]{3,2,1,0:T(8,128)S(1)} %fusion.87, f32[5,16,34,1]{3,2,1,0:T(8,128)S(1)} %copy-done.7, f32[5,16,1,128]{3,2,1,0:T(1,128)S(1)} %collective-permute-done.5, f32[5,16,1,128]{3,2,1,0:T(1,128)S(1)} %collective-permute-done.4, ...), kind=kLoop, calls=%fused_computation.143 | loop fusion | flops 19660800 | bytes 12076984 | tf_op jit(solution)/shard_map/vmap()/sub | solution.py:76
  282.1 5.1 %collective-permute-start.11 = (f32[5,16,34,1]{2,1,3,0:T(8,128)S(1)}, f32[5,16,34,1]{2,1,3,0:T(8,128)S(1)}, u32[]{:S(2)}, u32[]{:S(2)}) collective-permute-start(f32[5,16,34,1]{2,1,3,0:T(8,128)S(1)} %copy.169), channel_id=1, source_target_pairs={{1,0},{2,1},{3,2},{4,3},{5,4},{6,5},{7,6},{0,7},{9,8},{10,9},{11,1... | collective-permute-start | bytes 32648 | tf_op jit(solution)/shard_map/ppermute | solution.py:21
  294.3 6.3 %fusion.37 = f32[5,16,32,128]{3,2,1,0:T(8,128)S(1)} fusion(f32[5,18,34,130]{3,2,1,0:T(8,128)S(1)} %broadcast_multiply_fusion.1, f32[5,16,32,128]{3,2,1,0:T(8,128)S(1)} %fusion.62, f32[5,16,34,1]{3,2,1,0:T(8,128)S(1)} %copy-done.8, f32[5,16,1,128]{3,2,1,0:T(1,128)S(1)} %collective-permute-done.9, f32[5,16,1,128]{3,2,1,0:T(1,128)S(1)} %collective-permute-done.8, ...), kind=kLoop, calls=%fused_computation.96 | loop fusion | flops 19660800 | bytes 12076984 | tf_op jit(solution)/shard_map/vmap()/sub | solution.py:76
  311.0 4.9 %collective-permute-start.15 = (f32[5,16,34,1]{2,1,3,0:T(8,128)S(1)}, f32[5,16,34,1]{2,1,3,0:T(8,128)S(1)}, u32[]{:S(2)}, u32[]{:S(2)}) collective-permute-start(f32[5,16,34,1]{2,1,3,0:T(8,128)S(1)} %copy.177), channel_id=1, source_target_pairs={{1,0},{2,1},{3,2},{4,3},{5,4},{6,5},{7,6},{0,7},{9,8},{10,9},{11,1... | collective-permute-start | bytes 32648 | tf_op jit(solution)/shard_map/ppermute | solution.py:21
  323.0 6.3 %fusion.12 = f32[5,16,32,128]{3,2,1,0:T(8,128)S(1)} fusion(f32[5,18,34,130]{3,2,1,0:T(8,128)S(1)} %broadcast_multiply_fusion, f32[5,16,32,128]{3,2,1,0:T(8,128)S(1)} %fusion.37, f32[5,16,34,1]{3,2,1,0:T(8,128)S(1)} %copy-done.2, f32[5,16,1,128]{3,2,1,0:T(1,128)S(1)} %collective-permute-done.13, f32[5,16,1,128]{3,2,1,0:T(1,128)S(1)} %collective-permute-done.12, ...), kind=kLoop, calls=%fused_computation.49 | loop fusion | flops 19660800 | bytes 12076984 | tf_op jit(solution)/shard_map/vmap()/sub | solution.py:76
  329.3 13.6 %reshape.350 = f32[5,2,8,4,8,16,8]{6,5,4,3,2,1,0:T(8,128)} reshape(f32[5,16,32,128]{3,2,1,0:T(8,128)S(1)} %fusion.12) | data formatting | bytes 2621440 | tf_op jit(solution)/shard_map/reshape | solution.py:43
  342.9 18.0 %copy.184 = f32[2,4,16,5,8,8,8]{2,1,0,6,5,4,3:T(4,128)} copy(f32[2,4,16,5,8,8,8]{6,2,5,1,4,0,3:T(8,128)} %bitcast.88) | data formatting | bytes 2621440 | tf_op jit(solution)/shard_map/transpose | solution.py:44
  361.0 8.9 %reshape.351 = f32[128,5,512]{0,2,1:T(8,128)S(1)} reshape(f32[2,4,16,5,8,8,8]{2,1,0,6,5,4,3:T(4,128)} %copy.184) | data formatting | bytes 2621440 | tf_op jit(solution)/shard_map/reshape | solution.py:44
  373.1 3.4 copy.186
  (142 shorter events, 91.7 us)
Async XLA Ops:
  3.5 8.0 %all-to-all-start.2 = ((s32[4,8,1]{1,2,0:T(1,128)}), s32[4,8,1]{1,2,0:T(1,128)S(1)}, u32[]{:S(2)}, u32[]{:S(2)}) async-start(s32[4,8,1]{1,2,0:T(1,128)} %bitcast.10), calls=%async_computation.2 | async-start | bytes 4096 | tf_op jit(solution)/shard_map/all_to_all | solution.py:130
  11.4 25.9 %all-to-all-start = ((s32[32,8,1]{1,2,0:T(1,128)}), s32[32,8,1]{1,2,0:T(1,128)S(1)}, u32[]{:S(2)}, u32[]{:S(2)}) async-start(s32[32,8,1]{1,2,0:T(1,128)} %bitcast), calls=%async_computation | async-start | bytes 32768 | tf_op jit(solution)/shard_map/all_to_all | solution.py:111
  37.3 6.0 %copy-start.9 = (f32[32,5,512]{2,0,1:T(8,128)S(1)}, f32[32,5,512]{2,0,1:T(8,128)}, u32[]{:S(2)}) copy-start(f32[32,5,512]{2,0,1:T(8,128)} %param.10) | copy-start | bytes 983044
  37.3 102.0 %all-to-all-start.1 = ((f32[256,5,512]{2,1,0:T(8,128)}), f32[256,5,512]{2,1,0:T(8,128)}, u32[]{:S(2)}, u32[]{:S(2)}) async-start(f32[256,5,512]{2,1,0:T(8,128)} %scatter_fusion), calls=%async_computation.1 | async-start | bytes 8388608 | tf_op jit(solution)/shard_map/all_to_all | solution.py:110
  43.5 4.1 %copy-start = (s32[1,128]{1,0:T(1,128)S(1)}, s32[1,128]{1,0:T(1,128)}, u32[]{:S(2)}) copy-start(s32[1,128]{1,0:T(1,128)} %param.9) | copy-start | bytes 1540
  139.3 72.7 %all-to-all-start.3 = ((f32[4,1,2560]{2,1,0:T(1,128)}), f32[4,1,2560]{2,1,0:T(1,128)S(1)}, u32[]{:S(2)}, u32[]{:S(2)}) async-start(f32[4,1,2560]{2,1,0:T(1,128)} %reshape.447), calls=%async_computation.3 | async-start | bytes 81920 | tf_op jit(solution)/shard_map/all_to_all | solution.py:145
  206.1 12.1 %collective-permute-start = (f32[5,16,1,128]{3,2,1,0:T(1,128)S(1)}, f32[5,16,1,128]{3,2,1,0:T(1,128)S(1)}, u32[]{:S(2)}, u32[]{:S(2)}) collective-permute-start(f32[5,16,1,128]{3,2,1,0:T(1,128)S(1)} %get-tuple-element.25), channel_id=1, source_target_pairs={{0,8},{8,16},{16,24},{24,0},{1,9},{9,17},{17,25},{25,1},{2,10},{10... | collective-permute-start | bytes 122888 | tf_op jit(solution)/shard_map/ppermute | solution.py:20
  206.6 11.6 %collective-permute-start.1 = (f32[5,16,1,128]{3,2,1,0:T(1,128)S(1)}, f32[5,16,1,128]{3,2,1,0:T(1,128)S(1)}, u32[]{:S(2)}, u32[]{:S(2)}) collective-permute-start(f32[5,16,1,128]{3,2,1,0:T(1,128)S(1)} %get-tuple-element.26), channel_id=1, source_target_pairs={{8,0},{16,8},{24,16},{0,24},{9,1},{17,9},{25,17},{1,25},{10,2},{18... | collective-permute-start | bytes 122888 | tf_op jit(solution)/shard_map/ppermute | solution.py:21
  222.7 7.2 %collective-permute-start.2 = (f32[5,16,34,1]{2,1,3,0:T(8,128)S(1)}, f32[5,16,34,1]{2,1,3,0:T(8,128)S(1)}, u32[]{:S(2)}, u32[]{:S(2)}) collective-permute-start(f32[5,16,34,1]{2,1,3,0:T(8,128)S(1)} %copy.152), channel_id=1, source_target_pairs={{0,1},{1,2},{2,3},{3,4},{4,5},{5,6},{6,7},{7,0},{8,9},{9,10},{10,1... | collective-permute-start | bytes 32648 | tf_op jit(solution)/shard_map/ppermute | solution.py:20
  225.0 6.8 %collective-permute-start.3 = (f32[5,16,34,1]{2,1,3,0:T(8,128)S(1)}, f32[5,16,34,1]{2,1,3,0:T(8,128)S(1)}, u32[]{:S(2)}, u32[]{:S(2)}) collective-permute-start(f32[5,16,34,1]{2,1,3,0:T(8,128)S(1)} %copy.153), channel_id=1, source_target_pairs={{1,0},{2,1},{3,2},{4,3},{5,4},{6,5},{7,6},{0,7},{9,8},{10,9},{11,1... | collective-permute-start | bytes 32648 | tf_op jit(solution)/shard_map/ppermute | solution.py:21
  235.2 1.9 copy-start.6
  243.5 3.5 collective-permute-start.4
  243.6 3.4 collective-permute-start.5
  251.5 6.9 %collective-permute-start.6 = (f32[5,16,34,1]{2,1,3,0:T(8,128)S(1)}, f32[5,16,34,1]{2,1,3,0:T(8,128)S(1)}, u32[]{:S(2)}, u32[]{:S(2)}) collective-permute-start(f32[5,16,34,1]{2,1,3,0:T(8,128)S(1)} %copy.160), channel_id=1, source_target_pairs={{0,1},{1,2},{2,3},{3,4},{4,5},{5,6},{6,7},{7,0},{8,9},{9,10},{10,1... | collective-permute-start | bytes 32648 | tf_op jit(solution)/shard_map/ppermute | solution.py:20
  253.7 6.6 %collective-permute-start.7 = (f32[5,16,34,1]{2,1,3,0:T(8,128)S(1)}, f32[5,16,34,1]{2,1,3,0:T(8,128)S(1)}, u32[]{:S(2)}, u32[]{:S(2)}) collective-permute-start(f32[5,16,34,1]{2,1,3,0:T(8,128)S(1)} %copy.161), channel_id=1, source_target_pairs={{1,0},{2,1},{3,2},{4,3},{5,4},{6,5},{7,6},{0,7},{9,8},{10,9},{11,1... | collective-permute-start | bytes 32648 | tf_op jit(solution)/shard_map/ppermute | solution.py:21
  263.6 1.9 copy-start.7
  271.9 3.5 collective-permute-start.8
  273.7 1.7 collective-permute-start.9
  279.9 7.2 %collective-permute-start.10 = (f32[5,16,34,1]{2,1,3,0:T(8,128)S(1)}, f32[5,16,34,1]{2,1,3,0:T(8,128)S(1)}, u32[]{:S(2)}, u32[]{:S(2)}) collective-permute-start(f32[5,16,34,1]{2,1,3,0:T(8,128)S(1)} %copy.168), channel_id=1, source_target_pairs={{0,1},{1,2},{2,3},{3,4},{4,5},{5,6},{6,7},{7,0},{8,9},{9,10},{10,1... | collective-permute-start | bytes 32648 | tf_op jit(solution)/shard_map/ppermute | solution.py:20
  282.1 7.0 %collective-permute-start.11 = (f32[5,16,34,1]{2,1,3,0:T(8,128)S(1)}, f32[5,16,34,1]{2,1,3,0:T(8,128)S(1)}, u32[]{:S(2)}, u32[]{:S(2)}) collective-permute-start(f32[5,16,34,1]{2,1,3,0:T(8,128)S(1)} %copy.169), channel_id=1, source_target_pairs={{1,0},{2,1},{3,2},{4,3},{5,4},{6,5},{7,6},{0,7},{9,8},{10,9},{11,1... | collective-permute-start | bytes 32648 | tf_op jit(solution)/shard_map/ppermute | solution.py:21
  300.7 3.5 collective-permute-start.12
  302.6 1.7 collective-permute-start.13
  308.9 7.0 %collective-permute-start.14 = (f32[5,16,34,1]{2,1,3,0:T(8,128)S(1)}, f32[5,16,34,1]{2,1,3,0:T(8,128)S(1)}, u32[]{:S(2)}, u32[]{:S(2)}) collective-permute-start(f32[5,16,34,1]{2,1,3,0:T(8,128)S(1)} %copy.176), channel_id=1, source_target_pairs={{0,1},{1,2},{2,3},{3,4},{4,5},{5,6},{6,7},{7,0},{8,9},{9,10},{10,1... | collective-permute-start | bytes 32648 | tf_op jit(solution)/shard_map/ppermute | solution.py:20
  311.0 6.7 %collective-permute-start.15 = (f32[5,16,34,1]{2,1,3,0:T(8,128)S(1)}, f32[5,16,34,1]{2,1,3,0:T(8,128)S(1)}, u32[]{:S(2)}, u32[]{:S(2)}) collective-permute-start(f32[5,16,34,1]{2,1,3,0:T(8,128)S(1)} %copy.177), channel_id=1, source_target_pairs={{1,0},{2,1},{3,2},{4,3},{5,4},{6,5},{7,6},{0,7},{9,8},{10,9},{11,1... | collective-permute-start | bytes 32648 | tf_op jit(solution)/shard_map/ppermute | solution.py:21
  (8 other events, 11.7 us)
where the time goes:
time: 381 us; the launch traced here: 377 us
  local copies, waits for them, and re-layouts  192 us (50%)
  waiting for transfers between devices  96.3 us (25%)
  starting transfers between devices  46.2 us (12%)
  other arithmetic  37.6 us (10%)
  between operations  4.62 us (1%)
    all_to_all x1, waiting for transfers between devices, per_device(): lax.all_to_all(outgoing, ('gx', 'gy'), split_axis=0, concat_axis=0, tiled...  89.8 us
    sub x4, other arithmetic, update_field(): updated - (jnp.maximum(drift_speed, 0.0) * (middle - behind) + jnp.minimu...  25.1 us
    scatter x2, local copies, waits for them, and re-layouts, per_device(): jnp.zeros(fields_old.shape, jnp.float32).at[target]  22.9 us
    ppermute x8, starting transfers between devices, padded_2(): after = lax.ppermute(initial, axis, down)  22.6 us
    transpose x1, local copies, waits for them, and re-layouts, from_grid(): blocks.transpose(1, 3, 5, 0, 2, 4, 6)  18 us
    slice x12, local copies, waits for them, and re-layouts, padded_2(): last = lax.slice_in_dim(value, length - width, length, axis=dim)  17.3 us
    transpose x1, local copies, waits for them, and re-layouts, to_grid(): blocks.transpose(3, 0, 4, 1, 5, 2, 6)  17.3 us
    scatter x1, local copies, waits for them, and re-layouts, per_device(): jnp.zeros((devices * capacity,) + cell_shape, jnp.float32).at[position]  15.7 us
  transfers between devices with their start and end apart: 20, of which 6 were waited for; matrix products, arithmetic and copies ran while one was open for 30% of the time, Pallas kernels for 0%

commit v1 on v0

v1 whole, which is shorter than its diff:
```python
import functools

import jax
import jax.numpy as jnp
from jax import lax
from jax.experimental import pallas as pl
from jax.experimental.pallas import tpu as pltpu
from jax.sharding import PartitionSpec as P

S = 8
BX = 4
BY = 16
BZ = 2
SECTIONS = 4
F = 5
LANES = BX * BY * BZ
LAYER = S * S
CHUNKS = S * LAYER // LANES
VMEM_LIMIT = 56 * 1024 * 1024
MESH = pl.DeviceIdType.MESH
NN = (((1,), (0,)), ((), ()))
TN = (((0,), (0,)), ((), ()))
NT = (((1,), (1,)), ((), ()))


def iota(shape, axis):
    return lax.broadcasted_iota(jnp.int32, shape, axis)


def one_hot(mask):
    return jnp.where(mask, 1.0, 0.0).astype(jnp.bfloat16)


def parts(value):
    high = value.astype(jnp.bfloat16)
    rest = value - high.astype(jnp.float32)
    middle = rest.astype(jnp.bfloat16)
    low = (rest - middle.astype(jnp.float32)).astype(jnp.bfloat16)
    return high, middle, low


def pick(left, right, dims):
    def dot(a, b):
        return lax.dot_general(a, b, dims, preferred_element_type=jnp.float32)

    if left.dtype == jnp.float32:
        high, middle, low = (dot(part, right) for part in parts(left))
    else:
        high, middle, low = (dot(left, part) for part in parts(right))
    return high + middle + low


def roll(value, shift, axis):
    size = value.shape[axis]
    shift = shift % size
    return value if shift == 0 else pltpu.roll(value, shift, axis)


def pack_kernel(capacity, x_ref, row_ref, col_ref, send_ref):
    patches = x_ref.shape[0]
    slots = send_ref.shape[1]
    bits = patches.bit_length() - 1
    row, col = row_ref[...], col_ref[...]
    dest_row = lax.shift_right_logical(row, bits)
    dest_col = lax.shift_right_logical(col, bits)
    square = (patches, patches)
    before = (dest_col == dest_row) & (iota(square, 0) < iota(square, 1))
    count = jnp.sum(jnp.where(before, 1, 0), axis=0, keepdims=True)
    position = dest_row * capacity + count
    chosen = iota((slots, patches), 0) == position
    tag = ((row & (patches - 1)) + 1).astype(jnp.float32)
    tags = jnp.sum(jnp.where(chosen, tag, 0.0), axis=1, keepdims=True)
    send_ref[F * CHUNKS] = jnp.broadcast_to(tags, (slots, LANES))
    matrix = one_hot(chosen)
    for f in range(F):
        moved = pick(matrix, x_ref[:, f, :], NN)
        for c in range(CHUNKS):
            send_ref[f * CHUNKS + c] = moved[:, c * LANES : (c + 1) * LANES]


def sections_kernel(
    recv_ref, lane_ref, wall_ref, cand_ref, diff_ref, vel_ref, out_ref,
    cells, caps, cap_heat, grid_a, grid_b, heat,
    send_x, recv_x, send_y, recv_y, send_sem, recv_sem,
):
    gx, gy = lax.axis_index("gx"), lax.axis_index("gy")
    nx, ny = lax.axis_size("gx"), lax.axis_size("gy")
    right = (lax.rem(gx + 1, nx), gy)
    left = (lax.rem(gx + nx - 1, nx), gy)
    ahead = (gx, lax.rem(gy + 1, ny))
    behind = (gx, lax.rem(gy + ny - 1, ny))
    barrier = pltpu.get_barrier_semaphore()
    for other in (right, left, ahead, behind):
        pl.semaphore_signal(barrier, inc=1, device_id=other, device_id_type=MESH)

    slots = recv_ref.shape[1]
    lane = iota((S, LANES), 1)
    by = lane & (BY - 1)
    bz = lax.shift_right_logical(lane, 4) & 1
    bx = lax.shift_right_logical(lane, 5)
    level = iota((S, LANES), 0)

    tag_lane = (iota((slots, LANES), 1) + 1).astype(jnp.float32)
    tagged = one_hot(recv_ref[F * CHUNKS] == tag_lane)
    boxed = one_hot(lane_ref[...] == iota((LANES, LANES), 1))
    place = lax.dot_general(
        tagged, boxed, NN, preferred_element_type=jnp.float32
    ).astype(jnp.bfloat16)
    for f in range(F):
        for c in range(CHUNKS):
            cells[f, c * LANES : (c + 1) * LANES, :] = pick(
                recv_ref[f * CHUNKS + c], place, TN
            )
        for jk in range(LAYER):
            grid_a[f, jk // S + 1, jk % S + 1] = cells[f, pl.ds(jk, S, stride=LAYER), :]
    candidates = wall_ref.shape[1]
    named = one_hot(iota((candidates, LANES), 0) == cand_ref[...])
    row_lane = iota((1, LANES), 1)
    odd_y = (row_lane & 1) == 1
    odd_x = (lax.shift_right_logical(row_lane, 5) & 1) == 1
    top = (lax.shift_right_logical(row_lane, 4) & 1) == 1
    for f in range(F):
        both = pick(wall_ref[f], named, TN)
        side = jnp.where(top, both[LAYER:], both[:LAYER])
        half = jnp.where(odd_x, side[LAYER // 2 :], side[: LAYER // 2])
        for j2 in range(S // 2):
            for k2 in range(S // 2):
                at = j2 * S + k2
                row = jnp.where(odd_y, half[at + 4 : at + 5], half[at : at + 1])
                full = jnp.broadcast_to(row, (S, LANES))
                caps[f, j2, 2 * k2] = full
                caps[f, j2, 2 * k2 + 1] = full
    cap_heat[...] = 1.0 + 0.5 * jnp.tanh(caps[0])
    for a in (0, S + 1):
        for b in (0, S + 1):
            grid_a[0, a, b] = jnp.zeros((S, LANES), jnp.float32)
            grid_b[0, a, b] = jnp.zeros((S, LANES), jnp.float32)

    pl.semaphore_wait(barrier, 4)

    started = []
    for section in range(SECTIONS):
        now, later = (grid_a, grid_b) if section % 2 == 0 else (grid_b, grid_a)
        copies = []

        def send(src, dst, way, target):
            copy = pltpu.make_async_remote_copy(
                src_ref=src.at[section, way % 2],
                dst_ref=dst.at[section, way % 2],
                send_sem=send_sem.at[section, way],
                recv_sem=recv_sem.at[section, way],
                device_id=target,
                device_id_type=MESH,
            )
            copy.start()
            copies.append(copy)
            started.append(copy)

        for way, column, edge, target in ((2, S, BY - 1, ahead), (3, 1, 0, behind)):
            for q in range(-(-F * S // BY)):
                packed = jnp.zeros((S, LANES), jnp.float32)
                for r in range(BY):
                    n = q * BY + r
                    if n < F * S:
                        face = now[n // S, n % S + 1, column]
                        packed = jnp.where(by == r, roll(face, r - edge, 1), packed)
                send_y[section, way - 2, q] = packed
            send(send_y, recv_y, way, target)
        for way, plane, edge, target in ((0, S, BX - 1, right), (1, 1, 0, left)):
            for f in range(F):
                for q in range(S // BX):
                    packed = jnp.zeros((S, LANES), jnp.float32)
                    for g in range(BX):
                        face = now[f, plane, q * BX + g + 1]
                        moved = roll(face, (g - edge) * BY * BZ, 1)
                        packed = jnp.where(bx == g, moved, packed)
                    send_x[section, way, f * (S // BX) + q] = packed
            send(send_x, recv_x, way, target)

        for order, (way, column, target_column, edge, step) in enumerate(
            ((0, S, 0, 0, 1), (1, 1, S + 1, BY - 1, -1))
        ):
            copies[order].wait_recv()
            for n in range(F * S):
                q, r = n // BY, n % BY
                remote = roll(recv_y[section, way, q], edge - r, 1)
                local = roll(now[n // S, n % S + 1, column], step, 1)
                now[n // S, n % S + 1, target_column] = jnp.where(by == edge, remote, local)
        for order, (way, plane, target_plane, edge, step) in enumerate(
            ((0, S, 0, 0, 1), (1, 1, S + 1, BX - 1, -1))
        ):
            copies[2 + order].wait_recv()
            for f in range(F):
                for k in range(S):
                    q, g = k // BX, k % BX
                    packed = recv_x[section, way, f * (S // BX) + q]
                    remote = roll(packed, (edge - g) * BY * BZ, 1)
                    local = roll(now[f, plane, k + 1], step * BY * BZ, 1)
                    now[f, target_plane, k + 1] = jnp.where(bx == edge, remote, local)

        def warm(j, carry):
            heat[j] = 1.0 + 0.5 * jnp.tanh(now[0, j])
            return carry

        lax.fori_loop(0, S + 2, warm, 0)

        box = (S, S, LANES)
        is_top = (iota(box, 1) == S - 1)
        is_bottom = (iota(box, 1) == 0)
        bz3 = lax.shift_right_logical(iota(box, 2), 4) & 1

        def neighbours(value, cap):
            rolled = roll(value, -1, 1)
            outer = jnp.where(bz3 == 0, roll(rolled, -BY, 2), cap)
            above = jnp.where(is_top, outer, rolled)
            rolled = roll(value, 1, 1)
            outer = jnp.where(bz3 == 1, roll(rolled, BY, 2), cap)
            below = jnp.where(is_bottom, outer, rolled)
            return above, below

        def pair(j2, carry):
            for jr in range(2):
                j = 2 * j2 + jr + 1
                inner = slice(1, S + 1)
                here = heat[j, inner]
                warm_z = neighbours(here, cap_heat[j2])
                warm_x = heat[j + 1, inner], heat[j - 1, inner]
                warm_y = heat[j, 2 : S + 2], heat[j, 0:S]
                means = [
                    (0.5 * (here + up), 0.5 * (here + down))
                    for up, down in (warm_z, warm_x, warm_y)
                ]
                for f in range(F):
                    u = now[f, j, inner]
                    around = (
                        neighbours(u, caps[f, j2]),
                        (now[f, j + 1, inner], now[f, j - 1, inner]),
                        (now[f, j, 2 : S + 2], now[f, j, 0:S]),
                    )
                    total = u
                    for axis in range(3):
                        up, down = around[axis]
                        mean_up, mean_down = means[axis]
                        v = vel_ref[axis]
                        total = total + (diff_ref[f] * mean_up - jnp.minimum(v, 0.0)) * (up - u)
                        total = total - (diff_ref[f] * mean_down + jnp.maximum(v, 0.0)) * (u - down)
                    if section == SECTIONS - 1:
                        out_ref[f, j - 1] = total
                    else:
                        later[f, j, inner] = total
            return carry

        lax.fori_loop(0, S // 2, pair, 0)
    for copy in started:
        copy.wait_send()


def rows_kernel(grid_ref, lane_ref, out_ref):
    patches = lane_ref.shape[0]
    boxed = one_hot(lane_ref[...] == iota((patches, LANES), 1))
    for f in range(F):
        for c in range(CHUNKS):
            per = LANES // LAYER
            cells = jnp.concatenate(
                [grid_ref[f, pl.ds(c * per + i, LAYER, stride=S), :] for i in range(per)],
                axis=0,
            )
            out_ref[:, f, c * LANES : (c + 1) * LANES] = pick_rows(boxed, cells)


def pick_rows(boxed, cells):
    return pick(boxed, cells, NT)


def vmem(count):
    return [pl.BlockSpec(memory_space=pltpu.VMEM)] * count


def per_device(
    fields_old, new_place, box_slot, coarse_fields, coarse_source, diffusivity, velocity
):
    devices = lax.axis_size(("gx", "gy"))
    mesh_x = lax.axis_size("gx")
    mesh_y = lax.axis_size("gy")
    patches = fields_old.shape[0]
    capacity = 2 * patches // devices
    slots = devices * capacity
    tiles = F * CHUNKS + 1
    need = coarse_source.shape[1]
    f32 = jnp.float32

    packed = pl.pallas_call(
        functools.partial(pack_kernel, capacity),
        out_shape=jax.ShapeDtypeStruct((tiles, slots, LANES), f32),
        in_specs=vmem(3),
        out_specs=vmem(1)[0],
        compiler_params=pltpu.CompilerParams(vmem_limit_bytes=VMEM_LIMIT),
        name="pack",
    )(fields_old, new_place.reshape(1, patches), new_place.reshape(patches, 1))
    arrived = lax.all_to_all(packed, ("gx", "gy"), split_axis=1, concat_axis=1, tiled=True)

    top = S * LAYER
    below = 1.25 * coarse_fields[:, :, top - LAYER :] - 0.25 * coarse_fields[:, :, top - 2 * LAYER : top - LAYER]
    above = 1.25 * coarse_fields[:, :, :LAYER] - 0.25 * coarse_fields[:, :, LAYER : 2 * LAYER]
    walls = jnp.concatenate([below, above], axis=2).transpose(1, 0, 2)
    walls = lax.all_gather(walls, "gx", axis=1, tiled=True)

    box = box_slot[0]
    lane = ((box >> 4) & 3) * (BY * BZ) + (box >> 6) * BY + (box & 15)
    lane = lane.reshape(patches, 1)
    source = coarse_source[0]
    candidate = (source // need // mesh_y) * need + source % need
    candidate = candidate.reshape(2, BX // 2, BY // 2).transpose(1, 0, 2)
    candidate = jnp.broadcast_to(
        candidate[:, None, :, :, None], (BX // 2, 2, 2, BY // 2, 2)
    ).reshape(1, LANES)

    dma = pltpu.SemaphoreType.DMA((SECTIONS, 4))
    padded = pltpu.VMEM((F, S + 2, S + 2, S, LANES), f32)
    faces_x = pltpu.VMEM((SECTIONS, 2, F * S // BX, S, LANES), f32)
    faces_y = pltpu.VMEM((SECTIONS, 2, -(-F * S // BY), S, LANES), f32)
    smem = pl.BlockSpec(memory_space=pltpu.SMEM)
    grid = pl.pallas_call(
        sections_kernel,
        out_shape=jax.ShapeDtypeStruct((F, S, S, S, LANES), f32),
        in_specs=vmem(4) + [smem, smem],
        out_specs=vmem(1)[0],
        scratch_shapes=[
            pltpu.VMEM((F, S * LAYER, LANES), f32),
            pltpu.VMEM((F, S // 2, S, S, LANES), f32),
            pltpu.VMEM((S // 2, S, S, LANES), f32),
            padded,
            padded,
            pltpu.VMEM((S + 2, S + 2, S, LANES), f32),
            faces_x,
            faces_x,
            faces_y,
            faces_y,
            dma,
            dma,
        ],
        compiler_params=pltpu.CompilerParams(
            collective_id=1, has_side_effects=True, vmem_limit_bytes=VMEM_LIMIT
        ),
        name="sections",
    )(arrived, lane, walls, candidate, diffusivity, velocity)
    return pl.pallas_call(
        rows_kernel,
        out_shape=jax.ShapeDtypeStruct(fields_old.shape, f32),
        in_specs=vmem(2),
        out_specs=vmem(1)[0],
        compiler_params=pltpu.CompilerParams(vmem_limit_bytes=VMEM_LIMIT),
        name="rows",
    )(grid.reshape(F, LAYER * S, LANES), lane)


def solution(mesh):
    in_specs = (
        P(("gx", "gy"), None, None),
        P(("gx", "gy")),
        P(("gx", "gy"), None),
        P(("gx", "gy"), None, None),
        P(("gx", "gy"), None),
        P(),
        P(),
    )
    out_specs = P(("gx", "gy"), None, None)
    return jax.shard_map(
        per_device, mesh=mesh, in_specs=in_specs, out_specs=out_specs, check_vma=False
    )
```

time: 381 us -> 144 us (0.38); the launches traced: 377 us -> 144 us
  local copies, waits for them, and re-layouts: 192 us -> 16.9 us
  Pallas kernels: 0 us -> 48.6 us
  waiting for transfers between devices: 96.3 us -> 51.1 us
  starting transfers between devices: 46.2 us -> 7.3 us
  other arithmetic: 37.6 us -> 0.91 us
  blocking collectives: 0 us -> 18.8 us
  between operations: 4.62 us -> 0.07 us
    pallas_call x0 -> x3, Pallas kernels: none -> 48.6 us  [the longest x1 33.4 us: per_device(): pl.pallas_call(sections_kernel, out_shape=jax.ShapeDtypeStruct((F, S, S,...]
    reshape x9 -> x2, local copies, waits for them, and re-layouts: 49.1 us -> 1.48 us  [the longest x1 0.74 us: per_device(): new_place.reshape(patches, 1)]
    scatter x5 -> x0, local copies, waits for them, and re-layouts: 40.3 us -> none  [the longest x2 22.9 us: per_device(): jnp.zeros(fields_old.shape, jnp.float32).at[target]]
    all_to_all x4 -> x1, waiting for transfers between devices: 91.1 us -> 51.1 us  [per_device(): lax.all_to_all(packed, ('gx', 'gy'), split_axis=1, concat_axis=1, tiled=T...]
    transpose x3 -> x1, local copies, waits for them, and re-layouts: 37.3 us -> 0.01 us  [per_device(): candidate = candidate.reshape(2, BX // 2, BY // 2).transpose(1, 0, 2)]
    ppermute x16 -> x0, starting transfers between devices: 27.2 us -> none  [the longest x8 22.6 us: padded_2(): after = lax.ppermute(initial, axis, down)]
    slice x17 -> x0, local copies, waits for them, and re-layouts: 26.3 us -> none  [the longest x12 17.3 us: padded_2(): last = lax.slice_in_dim(value, length - width, length, axis=dim)]
    sub x5 -> x1, other arithmetic: 25.2 us -> 0.11 us  [per_device(): 1.25 * coarse_fields[:, :, top - LAYER:]]
  transfers between devices with their start and end apart: 20 -> 1, of which waited for: 6 -> 1; matrix products, arithmetic and copies ran while one was open for 30% -> 2% of each run, Pallas kernels for 0% -> 0%
where the time goes in v1:
time: 144 us
  waiting for transfers between devices  51.1 us (35%)
  Pallas kernels  48.6 us (34%)
  blocking collectives  18.8 us (13%)
  local copies, waits for them, and re-layouts  16.9 us (12%)
  starting transfers between devices  7.3 us (5%)
    all_to_all x1, waiting for transfers between devices, per_device(): lax.all_to_all(packed, ('gx', 'gy'), split_axis=1, concat_axis=1, tiled=T...  51.1 us
    pallas_call x1, Pallas kernels, per_device(): pl.pallas_call(sections_kernel, out_shape=jax.ShapeDtypeStruct((F, S, S,...  33.4 us
    all_gather x1, blocking collectives, per_device(): walls = lax.all_gather(walls, 'gx', axis=1, tiled=True)  18.8 us
    pallas_call x1, Pallas kernels, per_device(): pl.pallas_call(functools.partial(pack_kernel, capacity), out_shape=jax.Sh...  10.8 us
    all_to_all x1, starting transfers between devices, per_device(): lax.all_to_all(packed, ('gx', 'gy'), split_axis=1, concat_axis=1, tiled=T...  7.3 us
    pallas_call x1, local copies, waits for them, and re-layouts, per_device(): pl.pallas_call(functools.partial(pack_kernel, capacity), out_shape=jax.Sh...  5.04 us
    pallas_call x1, Pallas kernels, per_device(): pl.pallas_call(rows_kernel, out_shape=jax.ShapeDtypeStruct(fields_old.sha...  4.43 us
    unnamed x10, local copies, waits for them, and re-layouts  4.05 us
  transfers between devices with their start and end apart: 1, of which 1 were waited for; matrix products, arithmetic and copies ran while one was open for 2% of the time, Pallas kernels for 0%

profile of v1, /device:TPU:0, one launch (start us, length us, event | category | flops | bytes accessed | tf_op | source)
XLA Modules:
  0.0 143.7 jit_solution(15380718588216514933)
XLA Ops:
  0.0 0.0 copy-start.1
  0.0 3.5 %copy.20.x_ref = f32[128,5,512]{2,1,0:T(8,128)} copy(f32[128,5,512]{2,0,1:T(8,128)} %param.7) | data formatting | bytes 2621440 | tf_op args[0]
  3.5 0.0 copy-done.1
  3.5 0.7 copy.21.col_ref
  4.2 10.8 %pack.1 = f32[21,256,128]{2,1,0:T(8,128)} custom-call(f32[128,5,512]{2,1,0:T(8,128)} %copy.20.x_ref, s32[1,128]{1,0:T(1,128)} %bitcast.12, s32[128,1]{1,0:T(8,128)} %copy.21.col_ref), custom_call_target="tpu_custom_call" | custom-call | tf_op jit(solution)/shard_map/pack/pallas_call | solution.py:292
  15.0 5.0 %copy.22 = f32[21,256,128]{2,0,1:T(8,128)} copy(f32[21,256,128]{2,1,0:T(8,128)} %pack.1) | data formatting | bytes 5505024 | tf_op jit(solution)/shard_map/pack/pallas_call | solution.py:292
  20.1 7.3 %all-to-all-start = ((f32[21,256,128]{2,0,1:T(8,128)}), f32[21,256,128]{2,0,1:T(8,128)S(1)}, u32[]{:S(2)}, u32[]{:S(2)}) async-start(f32[21,256,128]{2,0,1:T(8,128)} %copy.22), calls=%async_computation | async-start | bytes 6291456 | tf_op jit(solution)/shard_map/all_to_all | solution.py:300
  27.4 0.0 copy-done.2
  27.4 0.7 copy.25.lane_ref
  28.1 0.6 broadcast.107
  28.7 0.0 copy-done.3
  28.7 0.7 reduce.3
  29.4 0.1 squeeze.4
  29.5 0.1 broadcast_in_dim.2
  29.6 0.7 reshape.74.cand_ref
  30.3 0.0 copy-done
  30.3 0.1 multiply_subtract_fusion.1
  30.4 0.1 maximum_bitcast_fusion
  30.5 18.8 %all_gather.3.wall_ref = f32[5,128,128]{2,1,0:T(8,128)} all-gather(f32[5,32,128]{2,1,0:T(8,128)S(1)} %maximum_bitcast_fusion), channel_id=1, replica_groups=mesh['gx'=4,'gy'=8] {'gx'}, dimensions={1}, use_global_device_ids=true | all-gather | bytes 409600 | tf_op jit(solution)/shard_map/all_gather | solution.py:306
  49.4 51.1 %all-to-all-done = f32[21,256,128]{2,0,1:T(8,128)S(1)} async-done(((f32[21,256,128]{2,0,1:T(8,128)}), f32[21,256,128]{2,0,1:T(8,128)S(1)}, u32[]{:S(2)}, u32[]{:S(2)}) %all-to-all-start) | async-done | bytes 2752544 | tf_op jit(solution)/shard_map/all_to_all | solution.py:300
  100.4 2.0 %copy.24.recv_ref = f32[21,256,128]{2,1,0:T(8,128)} copy(f32[21,256,128]{2,0,1:T(8,128)S(1)} %all-to-all-done) | data formatting | bytes 5505024 | tf_op jit(solution)/shard_map/all_to_all | solution.py:300
  102.5 33.4 %sections.1 = f32[5,8,8,8,128]{4,3,2,1,0:T(8,128)} custom-call(f32[21,256,128]{2,1,0:T(8,128)} %copy.24.recv_ref, s32[128,1]{1,0:T(8,128)} %copy.25.lane_ref, f32[5,128,128]{2,1,0:T(8,128)} %all_gather.3.wall_ref, s32[1,128]{1,0:T(1,128)} %reshape.74.cand_ref, f32[5]{0:T(128)} %diff_ref.1, f32[3]{0:T(128)} %vel_ref.1), custom_call_target="tpu_custom_call" | custom-call | tf_op jit(solution)/shard_map/sections/pallas_call | solution.py:323
  135.9 4.4 %rows.1 = f32[128,5,512]{2,1,0:T(8,128)} custom-call(f32[5,512,128]{2,1,0:T(8,128)} %bitcast.11, s32[128,1]{1,0:T(8,128)} %copy.25.lane_ref), custom_call_target="tpu_custom_call" | custom-call | tf_op jit(solution)/shard_map/rows/pallas_call | solution.py:347
  140.3 3.4 %copy.27 = f32[128,5,512]{2,0,1:T(8,128)} copy(f32[128,5,512]{2,1,0:T(8,128)} %rows.1) | data formatting | bytes 2621440 | tf_op jit(solution)/shard_map/rows/pallas_call | solution.py:347
  (6 shorter events, 0.0 us)
Async XLA Ops:
  0.0 3.5 %copy-start.1 = (s32[128]{0:T(128)S(1)}, s32[128]{0:T(128)}, u32[]{:S(2)}) copy-start(s32[128]{0:T(128)} %param.8) | copy-start | bytes 1540
  20.0 7.3 %copy-start.2 = (s32[1,128]{1,0:T(1,128)S(1)}, s32[1,128]{1,0:T(1,128)}, u32[]{:S(2)}) copy-start(s32[1,128]{1,0:T(1,128)} %param.9) | copy-start | bytes 1540
  20.0 8.6 %copy-start.3 = (s32[1,32]{1,0:T(1,128)S(1)}, s32[1,32]{1,0:T(1,128)}, u32[]{:S(2)}) copy-start(s32[1,32]{1,0:T(1,128)} %param.11) | copy-start | bytes 388
  20.1 10.3 %copy-start = (f32[32,5,512]{2,0,1:T(8,128)S(1)}, f32[32,5,512]{2,0,1:T(8,128)}, u32[]{:S(2)}) copy-start(f32[32,5,512]{2,0,1:T(8,128)} %param.10) | copy-start | bytes 983044
  20.1 80.4 %all-to-all-start = ((f32[21,256,128]{2,0,1:T(8,128)}), f32[21,256,128]{2,0,1:T(8,128)S(1)}, u32[]{:S(2)}, u32[]{:S(2)}) async-start(f32[21,256,128]{2,0,1:T(8,128)} %copy.22), calls=%async_computation | async-start | bytes 6291456 | tf_op jit(solution)/shard_map/all_to_all | solution.py:300

commit v2 on v1

--- a/solution.py
+++ b/solution.py
@@ -56,11 +56,9 @@
     return value if shift == 0 else pltpu.roll(value, shift, axis)
 
 
-def pack_kernel(capacity, x_ref, row_ref, col_ref, send_ref):
-    patches = x_ref.shape[0]
-    slots = send_ref.shape[1]
+def slot_matrix(capacity, slots, row, col):
+    patches = row.shape[1]
     bits = patches.bit_length() - 1
-    row, col = row_ref[...], col_ref[...]
     dest_row = lax.shift_right_logical(row, bits)
     dest_col = lax.shift_right_logical(col, bits)
     square = (patches, patches)
@@ -70,12 +68,100 @@
     chosen = iota((slots, patches), 0) == position
     tag = ((row & (patches - 1)) + 1).astype(jnp.float32)
     tags = jnp.sum(jnp.where(chosen, tag, 0.0), axis=1, keepdims=True)
-    send_ref[F * CHUNKS] = jnp.broadcast_to(tags, (slots, LANES))
-    matrix = one_hot(chosen)
-    for f in range(F):
-        moved = pick(matrix, x_ref[:, f, :], NN)
+    return one_hot(chosen), jnp.broadcast_to(tags, (slots, LANES))
+
+
+def pack(capacity, x_ref, row_ref, col_ref, send_ref):
+    devices = send_ref.shape[0]
+    block = (devices, capacity, LANES)
+    matrix, tags = slot_matrix(capacity, devices * capacity, row_ref[...], col_ref[...])
+    send_ref[:, F * CHUNKS] = tags.reshape(block)
+    for f in range(F):
+        moved = pick(matrix, x_ref[f], NN)
         for c in range(CHUNKS):
-            send_ref[f * CHUNKS + c] = moved[:, c * LANES : (c + 1) * LANES]
+            send_ref[:, f * CHUNKS + c] = moved[:, c * LANES : (c + 1) * LANES].reshape(block)
+
+
+def layers(coarse_ref, f):
+    low = coarse_ref[f, :, :LANES]
+    high = coarse_ref[f, :, (CHUNKS - 1) * LANES :]
+    below = 1.25 * roll(high, LAYER, 1) - 0.25 * high
+    above = 1.25 * roll(low, LAYER, 1) - 0.25 * low
+    return jnp.where(iota(low.shape, 1) < LAYER, below, above)
+
+
+def pack_kernel(capacity, x_ref, row_ref, col_ref, coarse_ref, send_ref, wall_ref):
+    pack(capacity, x_ref, row_ref, col_ref, send_ref)
+    for f in range(F):
+        wall_ref[f] = layers(coarse_ref, f)
+
+
+def exchange_kernel(
+    capacity, x_ref, row_ref, col_ref, coarse_ref, recv_ref, walls_ref,
+    send, wall, send_sem, recv_sem, wall_send, wall_recv, local_sem,
+):
+    gx, gy = lax.axis_index("gx"), lax.axis_index("gy")
+    nx, ny = lax.axis_size("gx"), lax.axis_size("gy")
+    devices = nx * ny
+    me = gx * ny + gy
+    barrier = pltpu.get_barrier_semaphore()
+
+    def partner(k):
+        other = me ^ k
+        return other, (lax.div(other, ny), lax.rem(other, ny))
+
+    def greet(k, carry):
+        pl.semaphore_signal(barrier, inc=1, device_id=partner(k)[1], device_id_type=MESH)
+        return carry
+
+    lax.fori_loop(1, devices, greet, 0)
+    for f in range(F):
+        wall[f] = layers(coarse_ref, f)
+    pack(capacity, x_ref, row_ref, col_ref, send)
+    pl.semaphore_wait(barrier, devices - 1)
+
+    def message(k):
+        other, where = partner(k)
+        return pltpu.make_async_remote_copy(
+            src_ref=send.at[other],
+            dst_ref=recv_ref.at[me],
+            send_sem=send_sem.at[k],
+            recv_sem=recv_sem.at[k],
+            device_id=where,
+            device_id_type=MESH,
+        )
+
+    def wall_message(k):
+        return pltpu.make_async_remote_copy(
+            src_ref=wall,
+            dst_ref=walls_ref.at[gx],
+            send_sem=wall_send.at[k],
+            recv_sem=wall_recv.at[k],
+            device_id=(gx ^ k, gy),
+            device_id_type=MESH,
+        )
+
+    def begin(k, carry):
+        message(k).start()
+        return carry
+
+    lax.fori_loop(1, devices, begin, 0)
+    own = pltpu.make_async_copy(send.at[me], recv_ref.at[me], local_sem.at[0])
+    own_wall = pltpu.make_async_copy(wall, walls_ref.at[gx], local_sem.at[1])
+    own.start()
+    own_wall.start()
+    for k in range(1, nx):
+        wall_message(k).start()
+    for k in range(1, nx):
+        wall_message(k).wait()
+
+    def finish(k, carry):
+        message(k).wait()
+        return carry
+
+    lax.fori_loop(1, devices, finish, 0)
+    own.wait()
+    own_wall.wait()
 
 
 def sections_kernel(
@@ -93,7 +179,7 @@
     for other in (right, left, ahead, behind):
         pl.semaphore_signal(barrier, inc=1, device_id=other, device_id_type=MESH)
 
-    slots = recv_ref.shape[1]
+    slots = recv_ref.shape[0] * recv_ref.shape[2]
     lane = iota((S, LANES), 1)
     by = lane & (BY - 1)
     bz = lax.shift_right_logical(lane, 4) & 1
@@ -101,26 +187,24 @@
     level = iota((S, LANES), 0)
 
     tag_lane = (iota((slots, LANES), 1) + 1).astype(jnp.float32)
-    tagged = one_hot(recv_ref[F * CHUNKS] == tag_lane)
+    tagged = one_hot(recv_ref[:, F * CHUNKS].reshape(slots, LANES) == tag_lane)
     boxed = one_hot(lane_ref[...] == iota((LANES, LANES), 1))
-    place = lax.dot_general(
-        tagged, boxed, NN, preferred_element_type=jnp.float32
-    ).astype(jnp.bfloat16)
+    place = lax.dot_general(tagged, boxed, NN, preferred_element_type=jnp.float32)
+    place = place.T.astype(jnp.bfloat16)
     for f in range(F):
         for c in range(CHUNKS):
-            cells[f, c * LANES : (c + 1) * LANES, :] = pick(
-                recv_ref[f * CHUNKS + c], place, TN
-            )
+            rows = recv_ref[:, f * CHUNKS + c].reshape(slots, LANES)
+            cells[f, c * LANES : (c + 1) * LANES, :] = pick(place, rows, NN).T
         for jk in range(LAYER):
             grid_a[f, jk // S + 1, jk % S + 1] = cells[f, pl.ds(jk, S, stride=LAYER), :]
-    candidates = wall_ref.shape[1]
+    candidates = wall_ref.shape[0] * wall_ref.shape[2]
     named = one_hot(iota((candidates, LANES), 0) == cand_ref[...])
     row_lane = iota((1, LANES), 1)
     odd_y = (row_lane & 1) == 1
     odd_x = (lax.shift_right_logical(row_lane, 5) & 1) == 1
     top = (lax.shift_right_logical(row_lane, 4) & 1) == 1
     for f in range(F):
-        both = pick(wall_ref[f], named, TN)
+        both = pick(wall_ref[:, f].reshape(candidates, LANES), named, TN)
         side = jnp.where(top, both[LAYER:], both[:LAYER])
         half = jnp.where(odd_x, side[LAYER // 2 :], side[: LAYER // 2])
         for j2 in range(S // 2):
@@ -265,11 +349,7 @@
                 [grid_ref[f, pl.ds(c * per + i, LAYER, stride=S), :] for i in range(per)],
                 axis=0,
             )
-            out_ref[:, f, c * LANES : (c + 1) * LANES] = pick_rows(boxed, cells)
-
-
-def pick_rows(boxed, cells):
-    return pick(boxed, cells, NT)
+            out_ref[f, :, c * LANES : (c + 1) * LANES] = pick(boxed, cells, NT)
 
 
 def vmem(count):
@@ -284,26 +364,56 @@
     mesh_y = lax.axis_size("gy")
     patches = fields_old.shape[0]
     capacity = 2 * patches // devices
-    slots = devices * capacity
     tiles = F * CHUNKS + 1
     need = coarse_source.shape[1]
     f32 = jnp.float32
 
-    packed = pl.pallas_call(
-        functools.partial(pack_kernel, capacity),
-        out_shape=jax.ShapeDtypeStruct((tiles, slots, LANES), f32),
-        in_specs=vmem(3),
-        out_specs=vmem(1)[0],
-        compiler_params=pltpu.CompilerParams(vmem_limit_bytes=VMEM_LIMIT),
-        name="pack",
-    )(fields_old, new_place.reshape(1, patches), new_place.reshape(patches, 1))
-    arrived = lax.all_to_all(packed, ("gx", "gy"), split_axis=1, concat_axis=1, tiled=True)
-
-    top = S * LAYER
-    below = 1.25 * coarse_fields[:, :, top - LAYER :] - 0.25 * coarse_fields[:, :, top - 2 * LAYER : top - LAYER]
-    above = 1.25 * coarse_fields[:, :, :LAYER] - 0.25 * coarse_fields[:, :, LAYER : 2 * LAYER]
-    walls = jnp.concatenate([below, above], axis=2).transpose(1, 0, 2)
-    walls = lax.all_gather(walls, "gx", axis=1, tiled=True)
+    own = need
+    operands = (
+        fields_old.transpose(1, 0, 2),
+        new_place.reshape(1, patches),
+        new_place.reshape(patches, 1),
+        coarse_fields.transpose(1, 0, 2),
+    )
+    if capacity % 8 == 0 and devices & (devices - 1) == 0 and mesh_x & (mesh_x - 1) == 0:
+        any_space = pl.BlockSpec(memory_space=pl.ANY)
+        block = (devices, tiles, capacity, LANES)
+        arrived, walls = pl.pallas_call(
+            functools.partial(exchange_kernel, capacity),
+            out_shape=(
+                jax.ShapeDtypeStruct(block, f32),
+                jax.ShapeDtypeStruct((mesh_x, F, own, LANES), f32),
+            ),
+            in_specs=vmem(4),
+            out_specs=(any_space, any_space),
+            scratch_shapes=[
+                pltpu.VMEM(block, f32),
+                pltpu.VMEM((F, own, LANES), f32),
+                pltpu.SemaphoreType.DMA((devices,)),
+                pltpu.SemaphoreType.DMA((devices,)),
+                pltpu.SemaphoreType.DMA((mesh_x,)),
+                pltpu.SemaphoreType.DMA((mesh_x,)),
+                pltpu.SemaphoreType.DMA((2,)),
+            ],
+            compiler_params=pltpu.CompilerParams(
+                collective_id=2, has_side_effects=True, vmem_limit_bytes=VMEM_LIMIT
+            ),
+            name="exchange",
+        )(*operands)
+    else:
+        packed, walls = pl.pallas_call(
+            functools.partial(pack_kernel, capacity),
+            out_shape=(
+                jax.ShapeDtypeStruct((devices, tiles, capacity, LANES), f32),
+                jax.ShapeDtypeStruct((F, own, LANES), f32),
+            ),
+            in_specs=vmem(4),
+            out_specs=tuple(vmem(2)),
+            compiler_params=pltpu.CompilerParams(vmem_limit_bytes=VMEM_LIMIT),
+            name="pack",
+        )(*operands)
+        arrived = lax.all_to_all(packed, ("gx", "gy"), split_axis=0, concat_axis=0, tiled=True)
+        walls = lax.all_gather(walls, "gx", axis=0)
 
     box = box_slot[0]
     lane = ((box >> 4) & 3) * (BY * BZ) + (box >> 6) * BY + (box & 15)
@@ -344,14 +454,15 @@
         ),
         name="sections",
     )(arrived, lane, walls, candidate, diffusivity, velocity)
-    return pl.pallas_call(
+    rows = pl.pallas_call(
         rows_kernel,
-        out_shape=jax.ShapeDtypeStruct(fields_old.shape, f32),
+        out_shape=jax.ShapeDtypeStruct((F, patches, S * LAYER), f32),
         in_specs=vmem(2),
         out_specs=vmem(1)[0],
         compiler_params=pltpu.CompilerParams(vmem_limit_bytes=VMEM_LIMIT),
         name="rows",
     )(grid.reshape(F, LAYER * S, LANES), lane)
+    return rows.transpose(1, 0, 2)
 
 
 def solution(mesh):

time: 144 us -> 111 us (0.77)
  Pallas kernels: 48.6 us -> 105 us
  waiting for transfers between devices: 51.1 us -> 0 us
  blocking collectives: 18.8 us -> 0 us
  local copies, waits for them, and re-layouts: 16.9 us -> 3.44 us
  starting transfers between devices: 7.3 us -> 0 us
    pallas_call x2, Pallas kernels: 15.2 us -> 69.6 us  [the longest x1 65.7 us: per_device(): pl.pallas_call(functools.partial(exchange_kernel, capacity), out_shape=(j...]
    all_to_all x1 -> x0, waiting for transfers between devices: 51.1 us -> none  [per_device(): lax.all_to_all(packed, ('gx', 'gy'), split_axis=1, concat_axis=1, tiled=T...]
    all_gather x1 -> x0, blocking collectives: 18.8 us -> none  [per_device(): walls = lax.all_gather(walls, 'gx', axis=1, tiled=True)]
    pallas_call x2 -> x0, local copies, waits for them, and re-layouts: 8.45 us -> none  [the longest x1 5.04 us: per_device(): pl.pallas_call(functools.partial(pack_kernel, capacity), out_shape=jax.Sh...]
    all_to_all x1 -> x0, starting transfers between devices: 7.3 us -> none  [per_device(): lax.all_to_all(packed, ('gx', 'gy'), split_axis=1, concat_axis=1, tiled=T...]
    unnamed x10 -> x1, local copies, waits for them, and re-layouts: 4.05 us -> 0.51 us
    pallas_call x1, Pallas kernels: 33.4 us -> 35.7 us  [per_device(): pl.pallas_call(sections_kernel, out_shape=jax.ShapeDtypeStruct((F, S, S,...]
    all_to_all x1 -> x0, local copies, waits for them, and re-layouts: 2.05 us -> none  [per_device(): lax.all_to_all(packed, ('gx', 'gy'), split_axis=1, concat_axis=1, tiled=T...]
  transfers between devices with their start and end apart: 1 -> 0, of which waited for: 1 -> 0; matrix products, arithmetic and copies ran while one was open for 2% -> 0% of each run, Pallas kernels for 0% -> 0%
where the time goes in v2:
time: 111 us
  Pallas kernels  105 us (95%)
  local copies, waits for them, and re-layouts  3.44 us (3%)
  other arithmetic  2 us (2%)
    pallas_call x1, Pallas kernels, per_device(): pl.pallas_call(functools.partial(exchange_kernel, capacity), out_shape=(j...  65.7 us
    pallas_call x1, Pallas kernels, per_device(): pl.pallas_call(sections_kernel, out_shape=jax.ShapeDtypeStruct((F, S, S,...  35.7 us
    pallas_call x1, Pallas kernels, per_device(): pl.pallas_call(rows_kernel, out_shape=jax.ShapeDtypeStruct((F, patches, S...  3.9 us

profile of v2, /device:TPU:0, one launch (start us, length us, event | category | flops | bytes accessed | tf_op | source)
XLA Modules:
  0.0 110.8 jit_solution(15058458417642817969)
XLA Ops:
  0.0 0.5 broadcast.95
  0.5 1.3 %reduce.3 = s32[32]{0:T(128)S(1)} reduce(s32[1,32]{1,0:T(1,128)} %param.11, s32[]{:T(128)} %broadcast.95), dimensions={0}, to_apply=%param.11.reduce_sub_computation.3 | reduce | bytes 260 | tf_op args[4]
  1.8 0.7 add_bitcast_fusion
  2.5 0.1 squeeze.4
  2.6 0.1 broadcast_in_dim.2
  2.7 0.7 reshape.74.cand_ref
  3.3 0.7 copy.14.lane_ref
  4.1 1.4 %copy.12.col_ref = s32[128,1]{1,0:T(8,128)} copy(s32[128,1]{0,1:T(1,128)} %bitcast.15) | data formatting | bytes 1024 | tf_op jit(solution)/shard_map/reshape | solution.py:375
  5.5 65.7 %exchange.1 = (f32[32,21,8,128]{3,2,1,0:T(8,128)}, f32[4,5,32,128]{3,2,1,0:T(8,128)}) custom-call(f32[5,128,512]{2,1,0:T(8,128)} %bitcast.13, s32[1,128]{1,0:T(1,128)} %bitcast.16, s32[128,1]{1,0:T(8,128)} %copy.12.col_ref, f32[5,32,512]{2,1,0:T(8,128)} %bitcast.14), custom_call_target="tpu_custom_call" | custom-call | tf_op jit(solution)/shard_map/exchange/pallas_call | solution.py:381
  71.2 35.7 %sections.1 = f32[5,8,8,8,128]{4,3,2,1,0:T(8,128)} custom-call(f32[32,21,8,128]{3,2,1,0:T(8,128)} %get-tuple-element.7.recv_ref, s32[128,1]{1,0:T(8,128)} %copy.14.lane_ref, f32[4,5,32,128]{3,2,1,0:T(8,128)} %get-tuple-element.8.wall_ref, s32[1,128]{1,0:T(1,128)} %reshape.74.cand_ref, f32[5]{0:T(128)} %diff_ref.1, f32[3]{0:T(128)} %vel_ref.1), custom_call_target="tpu_custom_call" | custom-call | tf_op jit(solution)/shard_map/sections/pallas_call | solution.py:433
  106.9 3.9 %rows.1 = f32[5,128,512]{2,1,0:T(8,128)} custom-call(f32[5,512,128]{2,1,0:T(8,128)} %bitcast.12, s32[128,1]{1,0:T(8,128)} %copy.14.lane_ref), custom_call_target="tpu_custom_call" | custom-call | tf_op jit(solution)/shard_map/rows/pallas_call | solution.py:457
  (2 shorter events, 0.0 us)

commit v3 on v1

v3 whole, which is shorter than its diff:
```python
import functools

import jax
import jax.numpy as jnp
from jax import lax
from jax.experimental import pallas as pl
from jax.experimental.pallas import tpu as pltpu
from jax.sharding import PartitionSpec as P

S = 8
BX = 4
BY = 16
BZ = 2
SECTIONS = 4
F = 5
LANES = BX * BY * BZ
LAYER = S * S
CHUNKS = S * LAYER // LANES
VMEM_LIMIT = 56 * 1024 * 1024
MESH = pl.DeviceIdType.MESH
NN = (((1,), (0,)), ((), ()))
TN = (((0,), (0,)), ((), ()))
NT = (((1,), (1,)), ((), ()))


def iota(shape, axis):
    return lax.broadcasted_iota(jnp.int32, shape, axis)


def one_hot(mask):
    return jnp.where(mask, 1.0, 0.0).astype(jnp.bfloat16)


def parts(value):
    high = value.astype(jnp.bfloat16)
    rest = value - high.astype(jnp.float32)
    middle = rest.astype(jnp.bfloat16)
    low = (rest - middle.astype(jnp.float32)).astype(jnp.bfloat16)
    return high, middle, low


def pick(left, right, dims):
    def dot(a, b):
        return lax.dot_general(a, b, dims, preferred_element_type=jnp.float32)

    if left.dtype == jnp.float32:
        high, middle, low = (dot(part, right) for part in parts(left))
    else:
        high, middle, low = (dot(left, part) for part in parts(right))
    return high + middle + low


def roll(value, shift, axis):
    size = value.shape[axis]
    shift = shift % size
    return value if shift == 0 else pltpu.roll(value, shift, axis)


def column(row):
    wide = jnp.broadcast_to(row.astype(jnp.float32), (row.shape[1], row.shape[1]))
    return wide.T.astype(jnp.int32)


def slot_matrix(capacity, slots, row):
    patches = row.shape[1]
    bits = patches.bit_length() - 1
    dest_row = lax.shift_right_logical(row, bits)
    dest_col = lax.shift_right_logical(column(row), bits)
    square = (patches, patches)
    before = (dest_col == dest_row) & (iota(square, 0) < iota(square, 1))
    count = jnp.sum(jnp.where(before, 1, 0), axis=0, keepdims=True)
    return one_hot(iota((slots, patches), 0) == dest_row * capacity + count)


def pack(matrix, x_ref, send_ref, f):
    _, devices, _, capacity, _ = send_ref.shape
    moved = pick(matrix, x_ref[f], NN)
    for c in range(CHUNKS):
        part = moved[:, c * LANES : (c + 1) * LANES]
        send_ref[f, :, c] = part.reshape(devices, capacity, LANES)


def layers(coarse_ref, f):
    low = coarse_ref[f, :, :LANES]
    high = coarse_ref[f, :, (CHUNKS - 1) * LANES :]
    below = 1.25 * roll(high, LAYER, 1) - 0.25 * high
    above = 1.25 * roll(low, LAYER, 1) - 0.25 * low
    return jnp.where(iota(low.shape, 1) < LAYER, below, above)


def pack_kernel(x_ref, row_ref, coarse_ref, send_ref, wall_ref):
    _, devices, _, capacity, _ = send_ref.shape
    matrix = slot_matrix(capacity, devices * capacity, row_ref[...])
    for f in range(F):
        pack(matrix, x_ref, send_ref, f)
        wall_ref[f] = layers(coarse_ref, f)


def box_lane(box):
    across = lax.shift_right_logical(box, 4) & (BX - 1)
    return across * (BY * BZ) + lax.shift_right_logical(box, 6) * BY + (box & (BY - 1))


def local_kernel(recv_ref, rows_ref, wall_ref, *rest):
    sections(recv_ref, rows_ref, wall_ref, None, *rest)


def whole_kernel(
    x_ref, row_ref, coarse_ref, box_ref, source_ref, diff_ref, vel_ref, out_ref,
    send, recv, rows, wall, walls, send_sem, recv_sem, row_send, row_recv,
    wall_send, wall_recv, own_sem, *rest,
):
    gx, gy = lax.axis_index("gx"), lax.axis_index("gy")
    nx, ny = lax.axis_size("gx"), lax.axis_size("gy")
    devices = nx * ny
    capacity = send.shape[3]
    me = gx * ny + gy
    barrier = pltpu.get_barrier_semaphore()

    def partner(k):
        other = me ^ k
        return other, (lax.div(other, ny), lax.rem(other, ny))

    def each(body):
        def step(k, carry):
            body(k)
            return carry

        lax.fori_loop(1, devices, step, 0)

    def greet(k):
        pl.semaphore_signal(barrier, inc=1, device_id=partner(k)[1], device_id_type=MESH)

    each(greet)
    matrix = slot_matrix(capacity, devices * capacity, row_ref[...])
    pack(matrix, x_ref, send, 0)
    pl.semaphore_wait(barrier, devices - 1)

    def message(f, k):
        other, where = partner(k)
        return pltpu.make_async_remote_copy(
            src_ref=send.at[f, other],
            dst_ref=recv.at[f, me],
            send_sem=send_sem.at[f, k],
            recv_sem=recv_sem.at[f, k],
            device_id=where,
            device_id_type=MESH,
        )

    def row_message(k):
        return pltpu.make_async_remote_copy(
            src_ref=row_ref,
            dst_ref=rows.at[me],
            send_sem=row_send.at[k],
            recv_sem=row_recv.at[k],
            device_id=partner(k)[1],
            device_id_type=MESH,
        )

    def wall_message(k):
        return pltpu.make_async_remote_copy(
            src_ref=wall,
            dst_ref=walls.at[gx],
            send_sem=wall_send.at[k],
            recv_sem=wall_recv.at[k],
            device_id=(gx ^ k, gy),
            device_id_type=MESH,
        )

    def own(f):
        return pltpu.make_async_copy(send.at[f, me], recv.at[f, me], own_sem.at[f])

    own_row = pltpu.make_async_copy(row_ref, rows.at[me], own_sem.at[F])
    own_wall = pltpu.make_async_copy(wall, walls.at[gx], own_sem.at[F + 1])
    own_row.start()
    for f in range(F):
        if f:
            pack(matrix, x_ref, send, f)
        each(lambda k: message(f, k).start())
        own(f).start()
        if f == 0:
            each(lambda k: row_message(k).start())
            for g in range(F):
                wall[g] = layers(coarse_ref, g)
            for k in range(1, nx):
                wall_message(k).start()
            own_wall.start()

    def ready(what):
        if what == "rows":
            each(lambda k: row_message(k).wait())
            own_row.wait()
        elif what == "walls":
            for k in range(1, nx):
                wall_message(k).wait()
            own_wall.wait()
        else:
            each(lambda k: message(what, k).wait())
            own(what).wait()

    sections(
        recv, rows, walls, ready, box_ref, source_ref, diff_ref, vel_ref, out_ref, *rest
    )


def sections(
    recv_ref, rows_ref, wall_ref, ready, box_ref, source_ref, diff_ref, vel_ref, out_ref,
    cells, caps, cap_heat, grid_a, grid_b, heat,
    send_x, recv_x, send_y, recv_y, face_send, face_recv,
):
    gx, gy = lax.axis_index("gx"), lax.axis_index("gy")
    nx, ny = lax.axis_size("gx"), lax.axis_size("gy")
    me = gx * ny + gy
    right = (lax.rem(gx + 1, nx), gy)
    left = (lax.rem(gx + nx - 1, nx), gy)
    ahead = (gx, lax.rem(gy + 1, ny))
    behind = (gx, lax.rem(gy + ny - 1, ny))
    if ready is None:
        barrier = pltpu.get_barrier_semaphore()
        for other in (right, left, ahead, behind):
            pl.semaphore_signal(barrier, inc=1, device_id=other, device_id_type=MESH)
        pl.semaphore_wait(barrier, 4)

        def ready(what):
            return None

    _, devices, _, capacity, _ = recv_ref.shape
    slots = devices * capacity
    patches = LANES
    bits = patches.bit_length() - 1
    lane = iota((S, LANES), 1)
    by = lane & (BY - 1)
    bz = lax.shift_right_logical(lane, 4) & 1
    bx = lax.shift_right_logical(lane, 5)

    ready("walls")
    candidates = wall_ref.shape[0] * wall_ref.shape[2]
    need = wall_ref.shape[2]
    row_lane = iota((1, LANES), 1)
    entry = (
        (lax.shift_right_logical(row_lane, 4) & 1) * (need // 2)
        + lax.shift_right_logical(row_lane, 6) * (BY // 2)
        + lax.shift_right_logical(row_lane & (BY - 1), 1)
    )
    source = jnp.zeros((1, LANES), jnp.int32)
    for m in range(need):
        source = jnp.where(entry == m, source_ref[0, m], source)
    low_bits = need.bit_length() - 1
    owner = lax.shift_right_logical(source, low_bits + ny.bit_length() - 1)
    named = one_hot(iota((candidates, LANES), 0) == owner * need + (source & (need - 1)))
    odd_y = (row_lane & 1) == 1
    odd_x = (lax.shift_right_logical(row_lane, 5) & 1) == 1
    top = (lax.shift_right_logical(row_lane, 4) & 1) == 1
    for f in range(F):
        both = pick(wall_ref[:, f].reshape(candidates, LANES), named, TN)
        side = jnp.where(top, both[LAYER:], both[:LAYER])
        half = jnp.where(odd_x, side[LAYER // 2 :], side[: LAYER // 2])
        for j2 in range(S // 2):
            for k2 in range(S // 2):
                at = j2 * S + k2
                row = jnp.where(odd_y, half[at + 4 : at + 5], half[at : at + 1])
                full = jnp.broadcast_to(row, (S, LANES))
                caps[f, j2, 2 * k2] = full
                caps[f, j2, 2 * k2 + 1] = full
    cap_heat[...] = 1.0 + 0.5 * jnp.tanh(caps[0])
    for a in (0, S + 1):
        for b in (0, S + 1):
            grid_a[0, a, b] = jnp.zeros((S, LANES), jnp.float32)
            grid_b[0, a, b] = jnp.zeros((S, LANES), jnp.float32)

    ready("rows")
    senders = rows_ref[...].reshape(devices, LANES)
    sender = lax.shift_right_logical(iota((slots, devices), 0), capacity.bit_length() - 1)
    expand = one_hot(sender == iota((slots, devices), 1))
    places = pick(expand, senders.astype(jnp.float32), NN).astype(jnp.int32)
    mine = lax.shift_right_logical(places, bits) == me
    square = (LANES, LANES)
    earlier = lax.dot_general(
        one_hot(mine), one_hot(iota(square, 0) < iota(square, 1)), NN,
        preferred_element_type=jnp.float32,
    ).astype(jnp.int32)
    chosen = mine & (earlier == (iota((slots, LANES), 0) & (capacity - 1)))
    tag = jnp.sum(
        jnp.where(chosen, (places & (patches - 1)) + 1, 0), axis=1, keepdims=True
    )
    tagged = one_hot(tag == iota((slots, LANES), 1) + 1)
    boxed = one_hot(column(box_lane(box_ref[...])) == iota(square, 1))
    place = lax.dot_general(tagged, boxed, NN, preferred_element_type=jnp.float32)
    place = place.T.astype(jnp.bfloat16)
    for f in range(F):
        ready(f)
        for c in range(CHUNKS):
            part = recv_ref[f, :, c].reshape(slots, LANES)
            cells[f, c * LANES : (c + 1) * LANES, :] = pick(place, part, NN).T
        for jk in range(LAYER):
            grid_a[f, jk // S + 1, jk % S + 1] = cells[f, pl.ds(jk, S, stride=LAYER), :]

    started = []
    for section in range(SECTIONS):
        now, later = (grid_a, grid_b) if section % 2 == 0 else (grid_b, grid_a)
        copies = []

        def send(src, dst, way, target):
            copy = pltpu.make_async_remote_copy(
                src_ref=src.at[section, way % 2],
                dst_ref=dst.at[section, way % 2],
                send_sem=face_send.at[section, way],
                recv_sem=face_recv.at[section, way],
                device_id=target,
                device_id_type=MESH,
            )
            copy.start()
            copies.append(copy)
            started.append(copy)

        for way, line, edge, target in ((2, S, BY - 1, ahead), (3, 1, 0, behind)):
            for q in range(-(-F * S // BY)):
                packed = jnp.zeros((S, LANES), jnp.float32)
                for r in range(BY):
                    n = q * BY + r
                    if n < F * S:
                        face = now[n // S, n % S + 1, line]
                        packed = jnp.where(by == r, roll(face, r - edge, 1), packed)
                send_y[section, way - 2, q] = packed
            send(send_y, recv_y, way, target)
        for way, plane, edge, target in ((0, S, BX - 1, right), (1, 1, 0, left)):
            for f in range(F):
                for q in range(S // BX):
                    packed = jnp.zeros((S, LANES), jnp.float32)
                    for g in range(BX):
                        face = now[f, plane, q * BX + g + 1]
                        moved = roll(face, (g - edge) * BY * BZ, 1)
                        packed = jnp.where(bx == g, moved, packed)
                    send_x[section, way, f * (S // BX) + q] = packed
            send(send_x, recv_x, way, target)

        for order, (way, line, target_line, edge, step) in enumerate(
            ((0, S, 0, 0, 1), (1, 1, S + 1, BY - 1, -1))
        ):
            copies[order].wait_recv()
            for n in range(F * S):
                q, r = n // BY, n % BY
                remote = roll(recv_y[section, way, q], edge - r, 1)
                local = roll(now[n // S, n % S + 1, line], step, 1)
                now[n // S, n % S + 1, target_line] = jnp.where(by == edge, remote, local)
        for order, (way, plane, target_plane, edge, step) in enumerate(
            ((0, S, 0, 0, 1), (1, 1, S + 1, BX - 1, -1))
        ):
            copies[2 + order].wait_recv()
            for f in range(F):
                for k in range(S):
                    q, g = k // BX, k % BX
                    packed = recv_x[section, way, f * (S // BX) + q]
                    remote = roll(packed, (edge - g) * BY * BZ, 1)
                    local = roll(now[f, plane, k + 1], step * BY * BZ, 1)
                    now[f, target_plane, k + 1] = jnp.where(bx == edge, remote, local)

        def warm(j, carry):
            heat[j] = 1.0 + 0.5 * jnp.tanh(now[0, j])
            return carry

        lax.fori_loop(0, S + 2, warm, 0)

        box = (S, S, LANES)
        is_top = (iota(box, 1) == S - 1)
        is_bottom = (iota(box, 1) == 0)
        bz3 = lax.shift_right_logical(iota(box, 2), 4) & 1

        def neighbours(value, cap):
            rolled = roll(value, -1, 1)
            outer = jnp.where(bz3 == 0, roll(rolled, -BY, 2), cap)
            above = jnp.where(is_top, outer, rolled)
            rolled = roll(value, 1, 1)
            outer = jnp.where(bz3 == 1, roll(rolled, BY, 2), cap)
            below = jnp.where(is_bottom, outer, rolled)
            return above, below

        def pair(j2, carry):
            for jr in range(2):
                j = 2 * j2 + jr + 1
                inner = slice(1, S + 1)
                here = heat[j, inner]
                warm_z = neighbours(here, cap_heat[j2])
                warm_x = heat[j + 1, inner], heat[j - 1, inner]
                warm_y = heat[j, 2 : S + 2], heat[j, 0:S]
                means = [
                    (0.5 * (here + up), 0.5 * (here + down))
                    for up, down in (warm_z, warm_x, warm_y)
                ]
                for f in range(F):
                    u = now[f, j, inner]
                    around = (
                        neighbours(u, caps[f, j2]),
                        (now[f, j + 1, inner], now[f, j - 1, inner]),
                        (now[f, j, 2 : S + 2], now[f, j, 0:S]),
                    )
                    total = u
                    for axis in range(3):
                        up, down = around[axis]
                        mean_up, mean_down = means[axis]
                        v = vel_ref[axis]
                        total = total + (diff_ref[f] * mean_up - jnp.minimum(v, 0.0)) * (up - u)
                        total = total - (diff_ref[f] * mean_down + jnp.maximum(v, 0.0)) * (u - down)
                    if section == SECTIONS - 1:
                        out_ref[f, j - 1] = total
                    else:
                        later[f, j, inner] = total
            return carry

        lax.fori_loop(0, S // 2, pair, 0)
    for copy in started:
        copy.wait_send()


def rows_kernel(grid_ref, box_ref, out_ref):
    boxed = one_hot(column(box_lane(box_ref[...])) == iota((LANES, LANES), 1))
    for f in range(F):
        for c in range(CHUNKS):
            per = LANES // LAYER
            cells = jnp.concatenate(
                [grid_ref[f, pl.ds(c * per + i, LAYER, stride=S), :] for i in range(per)],
                axis=0,
            )
            out_ref[f, :, c * LANES : (c + 1) * LANES] = pick(boxed, cells, NT)


def vmem(count):
    return [pl.BlockSpec(memory_space=pltpu.VMEM)] * count


def per_device(
    fields_old, new_place, box_slot, coarse_fields, coarse_source, diffusivity, velocity
):
    devices = lax.axis_size(("gx", "gy"))
    mesh_x = lax.axis_size("gx")
    mesh_y = lax.axis_size("gy")
    patches = fields_old.shape[0]
    capacity = 2 * patches // devices
    need = coarse_source.shape[1]
    f32 = jnp.float32

    row = new_place.reshape(1, patches)
    operands = (fields_old.transpose(1, 0, 2), row, coarse_fields.transpose(1, 0, 2))
    shared = (box_slot, coarse_source, diffusivity, velocity)
    dma = pltpu.SemaphoreType.DMA
    padded = pltpu.VMEM((F, S + 2, S + 2, S, LANES), f32)
    faces_x = pltpu.VMEM((SECTIONS, 2, F * S // BX, S, LANES), f32)
    faces_y = pltpu.VMEM((SECTIONS, 2, -(-F * S // BY), S, LANES), f32)
    smem = pl.BlockSpec(memory_space=pltpu.SMEM)
    grid_shape = jax.ShapeDtypeStruct((F, S, S, S, LANES), f32)
    scratch = [
        pltpu.VMEM((F, S * LAYER, LANES), f32),
        pltpu.VMEM((F, S // 2, S, S, LANES), f32),
        pltpu.VMEM((S // 2, S, S, LANES), f32),
        padded,
        padded,
        pltpu.VMEM((S + 2, S + 2, S, LANES), f32),
        faces_x,
        faces_x,
        faces_y,
        faces_y,
        dma((SECTIONS, 4)),
        dma((SECTIONS, 4)),
    ]
    block = (F, devices, CHUNKS, capacity, LANES)
    params = pltpu.CompilerParams(
        collective_id=1, has_side_effects=True, vmem_limit_bytes=VMEM_LIMIT
    )
    if capacity % 8 == 0 and devices & (devices - 1) == 0 and mesh_x & (mesh_x - 1) == 0:
        grid = pl.pallas_call(
            whole_kernel,
            out_shape=grid_shape,
            in_specs=vmem(4) + [smem] * 3,
            out_specs=vmem(1)[0],
            scratch_shapes=[
                pltpu.VMEM(block, f32),
                pltpu.VMEM(block, f32),
                pltpu.VMEM((devices, 1, LANES), jnp.int32),
                pltpu.VMEM((F, need, LANES), f32),
                pltpu.VMEM((mesh_x, F, need, LANES), f32),
                dma((F, devices)),
                dma((F, devices)),
                dma((devices,)),
                dma((devices,)),
                dma((mesh_x,)),
                dma((mesh_x,)),
                dma((F + 2,)),
            ]
            + scratch,
            compiler_params=params,
            name="whole",
        )(*operands, *shared)
    else:
        packed, walls = pl.pallas_call(
            pack_kernel,
            out_shape=(
                jax.ShapeDtypeStruct(block, f32),
                jax.ShapeDtypeStruct((F, need, LANES), f32),
            ),
            in_specs=vmem(3),
            out_specs=tuple(vmem(2)),
            compiler_params=pltpu.CompilerParams(vmem_limit_bytes=VMEM_LIMIT),
            name="pack",
        )(*operands)
        arrived = lax.all_to_all(packed, ("gx", "gy"), split_axis=1, concat_axis=1, tiled=True)
        walls = lax.all_gather(walls, "gx", axis=0)
        rows_all = lax.all_gather(row, ("gx", "gy"), axis=0)
        grid = pl.pallas_call(
            local_kernel,
            out_shape=grid_shape,
            in_specs=vmem(4) + [smem] * 3,
            out_specs=vmem(1)[0],
            scratch_shapes=scratch,
            compiler_params=params,
            name="sections",
        )(arrived, rows_all, walls, *shared)
    rows = pl.pallas_call(
        rows_kernel,
        out_shape=jax.ShapeDtypeStruct((F, patches, S * LAYER), f32),
        in_specs=vmem(2),
        out_specs=vmem(1)[0],
        compiler_params=pltpu.CompilerParams(vmem_limit_bytes=VMEM_LIMIT),
        name="rows",
    )(grid.reshape(F, LAYER * S, LANES), box_slot)
    return rows.transpose(1, 0, 2)


def solution(mesh):
    in_specs = (
        P(("gx", "gy"), None, None),
        P(("gx", "gy")),
        P(("gx", "gy"), None),
        P(("gx", "gy"), None, None),
        P(("gx", "gy"), None),
        P(),
        P(),
    )
    out_specs = P(("gx", "gy"), None, None)
    return jax.shard_map(
        per_device, mesh=mesh, in_specs=in_specs, out_specs=out_specs, check_vma=False
    )
```

time: 144 us -> 103 us (0.72)
  Pallas kernels: 48.6 us -> 103 us
  waiting for transfers between devices: 51.1 us -> 0 us
  blocking collectives: 18.8 us -> 0 us
  local copies, waits for them, and re-layouts: 16.9 us -> 0 us
  starting transfers between devices: 7.3 us -> 0 us
    pallas_call x3 -> x2, Pallas kernels: 48.6 us -> 103 us  [the longest x1 99.2 us: per_device(): pl.pallas_call(whole_kernel, out_shape=grid_shape, in_specs=vmem(4) + [sm...]
    all_to_all x1 -> x0, waiting for transfers between devices: 51.1 us -> none  [per_device(): lax.all_to_all(packed, ('gx', 'gy'), split_axis=1, concat_axis=1, tiled=T...]
    all_gather x1 -> x0, blocking collectives: 18.8 us -> none  [per_device(): walls = lax.all_gather(walls, 'gx', axis=1, tiled=True)]
    pallas_call x2 -> x0, local copies, waits for them, and re-layouts: 8.45 us -> none  [the longest x1 5.04 us: per_device(): pl.pallas_call(functools.partial(pack_kernel, capacity), out_shape=jax.Sh...]
    all_to_all x1 -> x0, starting transfers between devices: 7.3 us -> none  [per_device(): lax.all_to_all(packed, ('gx', 'gy'), split_axis=1, concat_axis=1, tiled=T...]
    unnamed x10 -> x0, local copies, waits for them, and re-layouts: 4.05 us -> none
    all_to_all x1 -> x0, local copies, waits for them, and re-layouts: 2.05 us -> none  [per_device(): lax.all_to_all(packed, ('gx', 'gy'), split_axis=1, concat_axis=1, tiled=T...]
    reshape x2 -> x0, local copies, waits for them, and re-layouts: 1.48 us -> none  [the longest x1 0.74 us: per_device(): new_place.reshape(patches, 1)]
  transfers between devices with their start and end apart: 1 -> 0, of which waited for: 1 -> 0; matrix products, arithmetic and copies ran while one was open for 2% -> 0% of each run, Pallas kernels for 0% -> 0%
where the time goes in v3:
time: 103 us
  Pallas kernels  103 us (100%)
    pallas_call x1, Pallas kernels, per_device(): pl.pallas_call(whole_kernel, out_shape=grid_shape, in_specs=vmem(4) + [sm...  99.2 us
    pallas_call x1, Pallas kernels, per_device(): pl.pallas_call(rows_kernel, out_shape=jax.ShapeDtypeStruct((F, patches, S...  3.9 us

profile of v3, /device:TPU:0, one launch (start us, length us, event | category | flops | bytes accessed | tf_op | source)
XLA Modules:
  0.0 103.1 jit_solution(9808028004715454819)
XLA Ops:
  0.0 99.2 %whole.1 = f32[5,8,8,8,128]{4,3,2,1,0:T(8,128)} custom-call(f32[5,128,512]{2,1,0:T(8,128)} %bitcast.6, s32[1,128]{1,0:T(1,128)} %bitcast.8, f32[5,32,512]{2,1,0:T(8,128)} %bitcast.7, s32[1,128]{1,0:T(1,128)} %box_ref.3, s32[1,32]{1,0:T(1,128)} %source_ref.1, f32[5]{0:T(128)} %diff_ref.1, f32[3]{0:T(128)} %vel_ref.1), custom_call_target="tpu_custom_call" | custom-call | tf_op jit(solution)/shard_map/whole/pallas_call | solution.py:470
  99.2 3.9 %rows.1 = f32[5,128,512]{2,1,0:T(8,128)} custom-call(f32[5,512,128]{2,1,0:T(8,128)} %bitcast.5, s32[1,128]{1,0:T(1,128)} %box_ref.3), custom_call_target="tpu_custom_call" | custom-call | tf_op jit(solution)/shard_map/rows/pallas_call | solution.py:517

commit v4 on v3

--- a/solution.py
+++ b/solution.py
@@ -343,6 +343,61 @@
                 remote = roll(recv_y[section, way, q], edge - r, 1)
                 local = roll(now[n // S, n % S + 1, line], step, 1)
                 now[n // S, n % S + 1, target_line] = jnp.where(by == edge, remote, local)
+        def warm(j, carry):
+            heat[j] = 1.0 + 0.5 * jnp.tanh(now[0, j])
+            return carry
+
+        lax.fori_loop(1, S + 1, warm, 0)
+
+        box = (S, S, LANES)
+        is_top = (iota(box, 1) == S - 1)
+        is_bottom = (iota(box, 1) == 0)
+        bz3 = lax.shift_right_logical(iota(box, 2), 4) & 1
+
+        def neighbours(value, cap):
+            rolled = roll(value, -1, 1)
+            outer = jnp.where(bz3 == 0, roll(rolled, -BY, 2), cap)
+            above = jnp.where(is_top, outer, rolled)
+            rolled = roll(value, 1, 1)
+            outer = jnp.where(bz3 == 1, roll(rolled, BY, 2), cap)
+            below = jnp.where(is_bottom, outer, rolled)
+            return above, below
+
+        def update(j, j2):
+            inner = slice(1, S + 1)
+            here = heat[j, inner]
+            warm_z = neighbours(here, cap_heat[j2])
+            warm_x = heat[j + 1, inner], heat[j - 1, inner]
+            warm_y = heat[j, 2 : S + 2], heat[j, 0:S]
+            means = [
+                (0.5 * (here + up), 0.5 * (here + down))
+                for up, down in (warm_z, warm_x, warm_y)
+            ]
+            for f in range(F):
+                u = now[f, j, inner]
+                around = (
+                    neighbours(u, caps[f, j2]),
+                    (now[f, j + 1, inner], now[f, j - 1, inner]),
+                    (now[f, j, 2 : S + 2], now[f, j, 0:S]),
+                )
+                total = u
+                for axis in range(3):
+                    up, down = around[axis]
+                    mean_up, mean_down = means[axis]
+                    v = vel_ref[axis]
+                    total = total + (diff_ref[f] * mean_up - jnp.minimum(v, 0.0)) * (up - u)
+                    total = total - (diff_ref[f] * mean_down + jnp.maximum(v, 0.0)) * (u - down)
+                if section == SECTIONS - 1:
+                    out_ref[f, j - 1] = total
+                else:
+                    later[f, j, inner] = total
+
+        def pair(t, carry):
+            update(2 * t, t - 1)
+            update(2 * t + 1, t)
+            return carry
+
+        lax.fori_loop(1, S // 2, pair, 0)
         for order, (way, plane, target_plane, edge, step) in enumerate(
             ((0, S, 0, 0, 1), (1, 1, S + 1, BX - 1, -1))
         ):
@@ -355,59 +410,10 @@
                     local = roll(now[f, plane, k + 1], step * BY * BZ, 1)
                     now[f, target_plane, k + 1] = jnp.where(bx == edge, remote, local)
 
-        def warm(j, carry):
-            heat[j] = 1.0 + 0.5 * jnp.tanh(now[0, j])
-            return carry
-
-        lax.fori_loop(0, S + 2, warm, 0)
-
-        box = (S, S, LANES)
-        is_top = (iota(box, 1) == S - 1)
-        is_bottom = (iota(box, 1) == 0)
-        bz3 = lax.shift_right_logical(iota(box, 2), 4) & 1
-
-        def neighbours(value, cap):
-            rolled = roll(value, -1, 1)
-            outer = jnp.where(bz3 == 0, roll(rolled, -BY, 2), cap)
-            above = jnp.where(is_top, outer, rolled)
-            rolled = roll(value, 1, 1)
-            outer = jnp.where(bz3 == 1, roll(rolled, BY, 2), cap)
-            below = jnp.where(is_bottom, outer, rolled)
-            return above, below
-
-        def pair(j2, carry):
-            for jr in range(2):
-                j = 2 * j2 + jr + 1
-                inner = slice(1, S + 1)
-                here = heat[j, inner]
-                warm_z = neighbours(here, cap_heat[j2])
-                warm_x = heat[j + 1, inner], heat[j - 1, inner]
-                warm_y = heat[j, 2 : S + 2], heat[j, 0:S]
-                means = [
-                    (0.5 * (here + up), 0.5 * (here + down))
-                    for up, down in (warm_z, warm_x, warm_y)
-                ]
-                for f in range(F):
-                    u = now[f, j, inner]
-                    around = (
-                        neighbours(u, caps[f, j2]),
-                        (now[f, j + 1, inner], now[f, j - 1, inner]),
-                        (now[f, j, 2 : S + 2], now[f, j, 0:S]),
-                    )
-                    total = u
-                    for axis in range(3):
-                        up, down = around[axis]
-                        mean_up, mean_down = means[axis]
-                        v = vel_ref[axis]
-                        total = total + (diff_ref[f] * mean_up - jnp.minimum(v, 0.0)) * (up - u)
-                        total = total - (diff_ref[f] * mean_down + jnp.maximum(v, 0.0)) * (u - down)
-                    if section == SECTIONS - 1:
-                        out_ref[f, j - 1] = total
-                    else:
-                        later[f, j, inner] = total
-            return carry
-
-        lax.fori_loop(0, S // 2, pair, 0)
+        warm(0, 0)
+        warm(S + 1, 0)
+        update(1, 0)
+        update(S, S // 2 - 1)
     for copy in started:
         copy.wait_send()
 

time: 103 us -> 103 us (level)
  no operation moved by 1% of the time
where the time goes in v4:
time: 103 us
  Pallas kernels  103 us (100%)
    pallas_call x1, Pallas kernels, per_device(): pl.pallas_call(whole_kernel, out_shape=grid_shape, in_specs=vmem(4) + [sm...  98.6 us
    pallas_call x1, Pallas kernels, per_device(): pl.pallas_call(rows_kernel, out_shape=jax.ShapeDtypeStruct((F, patches, S...  3.9 us

profile of v4, /device:TPU:0, one launch (start us, length us, event | category | flops | bytes accessed | tf_op | source)
XLA Modules:
  0.0 102.6 jit_solution(8227606245318507609)
XLA Ops:
  0.0 98.6 %whole.1 = f32[5,8,8,8,128]{4,3,2,1,0:T(8,128)} custom-call(f32[5,128,512]{2,1,0:T(8,128)} %bitcast.6, s32[1,128]{1,0:T(1,128)} %bitcast.8, f32[5,32,512]{2,1,0:T(8,128)} %bitcast.7, s32[1,128]{1,0:T(1,128)} %box_ref.3, s32[1,32]{1,0:T(1,128)} %source_ref.1, f32[5]{0:T(128)} %diff_ref.1, f32[3]{0:T(128)} %vel_ref.1), custom_call_target="tpu_custom_call" | custom-call | tf_op jit(solution)/shard_map/whole/pallas_call | solution.py:476
  98.6 3.9 %rows.1 = f32[5,128,512]{2,1,0:T(8,128)} custom-call(f32[5,512,128]{2,1,0:T(8,128)} %bitcast.5, s32[1,128]{1,0:T(1,128)} %box_ref.3), custom_call_target="tpu_custom_call" | custom-call | tf_op jit(solution)/shard_map/rows/pallas_call | solution.py:523
